TPU v7x, 32 devices: a whole 2x2x4 slice. The times are simulated.
32 devices in a mesh: gx: 4 (over y, x), gy: 4 (over z), band: 2 (over core).
Axes of the slice: x: 2, y: 2, z: 4, core: 2. Of those that a mesh axis runs over, the one named last changes fastest.
Arguments:
- orbitals: float32 [32, 32, 32, 128], P('band', 'gx', 'gy'), may hold values from -6 to 6
- local_potential: float32 [32, 32, 128], P('gx', 'gy'), may hold values from -4 to 0
- atom_cell: int32 [4, 4, 2], P('gx', 'gy'), may hold values from 0 to 8191
- support_offset: int32 [3, 4, 4, 2, 512], P(None, 'gx', 'gy'), may hold values from -6 to 6
- projector: float32 [4, 4, 2, 4, 512], P('gx', 'gy'), may hold values from -0.5 to 0.5
- coupling: float32 [4, 4, 2, 4], P('gx', 'gy'), may hold values from 8 to 32
Outputs:
- orbitals_new: float32 [32, 32, 32, 128], P('band', 'gx', 'gy')
- residual: float32 [32, 32, 32, 128], P('band', 'gx', 'gy')
- subspace: float32 [32, 32], replicated
Inputs may be any that keep to these rules, and one draw needn't show every extreme that they name: Each domain owns exactly 2 atoms; atom_cell is x * 8 * 128 + y * 128 + z for the atom's cell (x, y, z) counted within its domain. `support_offset`: support points of one atom may repeat; they may lie in neighbouring domains or outside the grid.
All inputs are finite; a program needn't handle non-finite values.
Results may differ from a plain program's by a relative error of at most 0.0003.
Values sent between devices are 32-bit elements; how exact they have to be, the bound alone decides.
A program may use at most 64 MiB of HBM per device.

v0:
```python
import jax
import jax.numpy as jnp
from jax import lax
from jax.sharding import PartitionSpec as P

spacing = 0.4
low_edge = 6.0
top_edge = 150.0
stencil = (
    -5369.0 / 1800.0,
    12.0 / 7.0,
    -15.0 / 56.0,
    10.0 / 189.0,
    -1.0 / 112.0,
    2.0 / 1925.0,
    -1.0 / 16632.0,
)
highest = lax.Precision.HIGHEST


def with_halo(cells, sides, width):
    for axis, dim in sides:
        count = lax.axis_size(axis)
        ends = count - 1
        head = lax.slice_in_dim(cells, 0, width, axis=dim)
        tail = lax.slice_in_dim(cells, cells.shape[dim] - width, cells.shape[dim], axis=dim)
        cells = jnp.concatenate(
            [
                lax.ppermute(tail, axis, [(i, (i + 1) % count) for i in range(ends)]),
                cells,
                lax.ppermute(head, axis, [((i + 1) % count, i) for i in range(ends)]),
            ],
            axis=dim,
        )
    return cells


def kinetic_part(extended, orbital_block):
    size_x, size_y, size_z = (
        orbital_block.shape[1],
        orbital_block.shape[2],
        orbital_block.shape[3],
    )
    padded_z = jnp.pad(orbital_block, ((0, 0), (0, 0), (0, 0), (6, 6)))
    summed = 3.0 * stencil[0] * orbital_block
    for stride in range(1, 7):
        along_x = (
            extended[:, 6 + stride : 6 + stride + size_x, 6 : 6 + size_y]
            + extended[:, 6 - stride : 6 - stride + size_x, 6 : 6 + size_y]
        )
        along_y = (
            extended[:, 6 : 6 + size_x, 6 + stride : 6 + stride + size_y]
            + extended[:, 6 : 6 + size_x, 6 - stride : 6 - stride + size_y]
        )
        along_z = (
            padded_z[..., 6 + stride : 6 + stride + size_z]
            + padded_z[..., 6 - stride : 6 - stride + size_z]
        )
        summed = summed + stencil[stride] * (along_x + along_y + along_z)
    return -0.5 / spacing**2 * summed


def prepare_tables(atom_cell, support_offset, projector, size_x, size_y, size_z):
    home_cell = atom_cell[..., None]
    relative = jnp.stack(
        [
            home_cell // (size_y * size_z) + support_offset[0],
            home_cell // size_z % size_y + support_offset[1],
            home_cell % size_z + support_offset[2],
        ]
    )
    rel_near = with_halo(relative, (("gx", 1), ("gy", 2)), 1)
    beta_near = with_halo(projector, (("gx", 0), ("gy", 1)), 1)
    atom_count, proj_count = (projector.shape[2], projector.shape[3])
    cell_count = size_x * size_y * size_z
    frame_x = (lax.broadcasted_iota(jnp.int32, (3, 3, 1, 1), 0) - 1) * size_x
    frame_y = (lax.broadcasted_iota(jnp.int32, (3, 3, 1, 1), 1) - 1) * size_y
    coord_x = rel_near[0] + frame_x
    coord_y = rel_near[1] + frame_y
    coord_z = rel_near[2]
    inside = (
        (coord_x >= 0)
        & (coord_x < size_x)
        & (coord_y >= 0)
        & (coord_y < size_y)
        & (coord_z >= 0)
        & (coord_z < size_z)
    ).astype(jnp.float32)
    cell_index = (
        jnp.clip(coord_x, 0, size_x - 1) * size_y + jnp.clip(coord_y, 0, size_y - 1)
    ) * size_z + jnp.clip(coord_z, 0, size_z - 1)
    near_columns = jnp.arange(9 * atom_count * proj_count, dtype=jnp.int32).reshape(
        3, 3, atom_count, proj_count, 1
    )
    near_flat = near_columns * cell_count + cell_index[:, :, :, None, :]
    near_values = beta_near * inside[:, :, :, None, :]
    table_near = (
        jnp.zeros((9 * atom_count * proj_count * cell_count,), jnp.float32)
        .at[near_flat.reshape(-1)]
        .add(near_values.reshape(-1))
    )
    table_near = table_near.reshape(3, 3, atom_count, proj_count, cell_count)
    own_rel = relative[:, 0, 0]
    own_x = own_rel[0] + 6
    own_y = own_rel[1] + 6
    own_z = own_rel[2]
    own_zin = ((own_z >= 0) & (own_z < size_z)).astype(jnp.float32)
    own_index = (own_x * (size_y + 12) + own_y) * size_z + jnp.clip(own_z, 0, size_z - 1)
    ext_count = (size_x + 12) * (size_y + 12) * size_z
    own_columns = jnp.arange(atom_count * proj_count, dtype=jnp.int32).reshape(
        atom_count, proj_count, 1
    )
    own_flat = own_columns * ext_count + own_index[:, None, :]
    own_values = projector[0, 0] * own_zin[:, None, :]
    table_own = (
        jnp.zeros((atom_count * proj_count * ext_count,), jnp.float32)
        .at[own_flat.reshape(-1)]
        .add(own_values.reshape(-1))
    )
    table_own = table_own.reshape(atom_count, proj_count, ext_count)
    return (table_near, table_own)


def apply_hamiltonian(orbital_block, local_potential, tables, coupling_own):
    table_near, table_own = tables
    orb_count = orbital_block.shape[0]
    atom_count, proj_count = coupling_own.shape
    flat_block = orbital_block.reshape(orb_count, -1)
    extended = with_halo(orbital_block, (("gx", 1), ("gy", 2)), 6)
    kinetic = kinetic_part(extended, orbital_block)
    partial_terms = jnp.einsum("ijanc,bc->ijanb", table_near, flat_block, precision=highest)
    received = with_halo(partial_terms.reshape(1, 1, -1), (("gx", 0), ("gy", 1)), 1)
    grouped = received.reshape(3, 3, 3, 3, atom_count, proj_count, orb_count)
    coefficients = grouped[1, 1, 1, 1]
    for row_pos in range(3):
        for col_pos in range(3):
            if row_pos != 1 or col_pos != 1:
                coefficients = coefficients + grouped[row_pos, col_pos, 2 - row_pos, 2 - col_pos]
    scaled = coupling_own[:, :, None] * coefficients
    near_coefs = with_halo(scaled.reshape(1, 1, -1), (("gx", 0), ("gy", 1)), 1)
    near_coefs = near_coefs.reshape(3, 3, atom_count, proj_count, orb_count)
    projector_term = jnp.einsum("ijanc,ijanb->bc", table_near, near_coefs, precision=highest)
    return kinetic + local_potential * orbital_block + projector_term.reshape(orbital_block.shape)


def inverse_factor(intersection):
    factor = jnp.linalg.cholesky(intersection)
    identity = jnp.eye(intersection.shape[0], dtype=jnp.float32)
    return lax.linalg.triangular_solve(factor, identity, left_side=True, lower=True)


def per_device(orbitals, local_potential, atom_cell, support_offset, projector, coupling):
    orb_count, size_x, size_y, size_z = orbitals.shape
    tables = prepare_tables(atom_cell, support_offset, projector, size_x, size_y, size_z)
    coupling_own = coupling[0, 0]

    def hamiltonian(orbital_block):
        return apply_hamiltonian(orbital_block, local_potential, tables, coupling_own)

    middle = 0.5 * (top_edge + low_edge)
    half_width = 0.5 * (top_edge - low_edge)
    total_cells = float(size_x * size_y * size_z * lax.axis_size("gx") * lax.axis_size("gy"))
    band_start = lax.axis_index("band") * orb_count
    first_term = (hamiltonian(orbitals) - middle * orbitals) / half_width
    filtered = 2.0 * (hamiltonian(first_term) - middle * first_term) / half_width - orbitals
    filt_flat = filtered.reshape(orb_count, -1)
    orbs_all = orb_count * lax.axis_size("band")
    empty_square = jnp.zeros((orbs_all, orbs_all), jnp.float32)
    whole_block = lax.all_gather(filt_flat, "band", axis=0, tiled=True)
    over_cols = jnp.einsum("kc,lc->kl", whole_block, filt_flat, precision=highest) / total_cells
    intersection = lax.psum(
        lax.dynamic_update_slice(empty_square, over_cols, (0, band_start)), ("gx", "gy", "band")
    )
    inverse = inverse_factor(intersection)
    rotated_all = jnp.dot(inverse, whole_block, precision=highest)
    rotated = lax.dynamic_slice_in_dim(rotated_all, band_start, orb_count, 0)
    image_own = hamiltonian(rotated.reshape(orbitals.shape)).reshape(orb_count, -1)
    sub_cols = jnp.einsum("kc,lc->kl", rotated_all, image_own, precision=highest) / total_cells
    subspace = lax.psum(
        lax.dynamic_update_slice(empty_square, sub_cols, (0, band_start)), ("gx", "gy", "band")
    )
    cols_own = lax.dynamic_slice_in_dim(subspace, band_start, orb_count, 1)
    residual = (
        image_own - jnp.einsum("kl,kc->lc", cols_own, rotated_all, precision=highest)
    ) / half_width
    return (rotated.reshape(orbitals.shape), residual.reshape(orbitals.shape), subspace)


def solution(mesh):
    in_specs = (
        P("band", "gx", "gy", None),
        P("gx", "gy", None),
        P("gx", "gy", None),
        P(None, "gx", "gy", None, None),
        P("gx", "gy", None, None, None),
        P("gx", "gy", None, None),
    )
    out_specs = (P("band", "gx", "gy", None), P("band", "gx", "gy", None), P())
    return jax.shard_map(
        per_device, mesh=mesh, in_specs=in_specs, out_specs=out_specs, check_vma=False
    )
```

profile of v0, /device:TPU:0, one launch (start us, length us, event | category | flops | bytes accessed | tf_op | source)
XLA Modules:
  0.0 609.7 jit_solution(16649699281486597180)
XLA Ops:
  10.0 5.5 collective-permute-start.4
  15.5 4.8 collective-permute-start.8
  23.0 2.1 reshape.763
  26.4 4.5 collective-permute-start.6
  33.0 4.5 collective-permute-start.10
  39.4 232.5 %scatter_custom_fusion = f32[589824]{0:T(1024)} fusion(s32[36864]{0:T(1024)S(1)} %bitcast.141, f32[36864]{0:T(1024)S(1)} %bitcast.142, f32[]{:T(128)} %constant.122.clone.1), kind=kCustom, calls=%fused_computation.109 | custom fusion | flops 36864 | bytes 2359300 | tf_op jit(solution)/shard_map/scatter-add | solution.py:100
  271.9 2.7 reshape.727
  274.7 4.1 fusion.166
  278.9 3.5 collective-permute-start.12
  282.5 2.2 collective-permute-start.1
  287.3 14.0 %collective-permute-done.13 = f32[1,1,1152]{2,1,0:T(1,128)S(1)} collective-permute-done((f32[1,1,1152]{2,1,0:T(1,128)S(1)}, f32[1,1,1152]{2,1,0:T(1,128)S(1)}, u32[]{:S(2)}, u32[]{:S(2)}) %collective-permute-start.13) | collective-permute-done | bytes 4640 | tf_op jit(solution)/shard_map/ppermute | solution.py:31
  302.6 4.5 collective-permute-start.14
  312.7 2.9 collective-permute-start.3
  318.8 4.5 collective-permute-start.16
  325.9 11.8 %collective-permute-start.18 = (f32[3,1,128]{2,1,0:T(1,128)S(1)}, f32[3,1,128]{2,1,0:T(1,128)S(1)}, u32[]{:S(2)}, u32[]{:S(2)}) collective-permute-start(f32[3,1,128]{2,1,0:T(1,128)S(1)} %pad_maximum_fusion.14), channel_id=1, source_target_pairs={{0,2},{2,4},{4,6},{1,3},{3,5},{5,7},{8,10},{10,12},{12,14},{9,11},... | collective-permute-start | bytes 4616 | tf_op jit(solution)/shard_map/ppermute | solution.py:29
  337.7 2.7 reshape.773
  340.3 2.4 collective-permute-done.19
  342.9 6.4 %fusion.5 = f32[16,8,8,128,1,1,1]{3,0,6,4,1,2,5:T(8,128)S(1)} fusion(f32[8,8,128,2,3,3,4]{2,1,0,6,3,5,4:T(8,128)} %reshape.773, f32[3,3,2,4,16]{4,3,2,1,0:T(4,128)S(1)} %reshape.731), kind=kOutput, calls=%fused_computation.85 | convolution fusion | flops 113246208 | bytes 2888192 | tf_op jit(solution)/shard_map/ijanc,ijanb->bc/dot_general | solution.py:142
  349.3 9.5 %broadcast_multiply_fusion = (f32[16,8,8,128]{3,0,2,1:T(8,128)S(1)}, f32[16,8,8,128]{3,0,2,1:T(8,128)}) fusion(f32[16,8,8,128]{3,0,2,1:T(8,128)} %copy-done.5, f32[16,8,8,128,1,1,1]{3,0,6,4,1,2,5:T(8,128)S(1)} %fusion.5, f32[8,8,128]{2,1,0:T(8,128)S(1)} %copy-done.12, f32[16,20,8,128]{3,0,2,1:T(8,128)S(1)} %copy-done.1, ...), kind=kLoop, calls=%fused_computation.300 | loop fusion | flops 8126464 | bytes 11698176 | tf_op jit(solution)/shard_map/div | solution.py:164
  361.7 4.0 fusion.164
  365.8 2.9 collective-permute-start.24
  370.1 4.6 collective-permute-start.21
  377.3 4.5 collective-permute-start.26
  381.9 5.8 collective-permute-done.20
  390.7 5.5 collective-permute-start.23
  399.3 4.5 collective-permute-start.28
  406.5 4.7 collective-permute-start.30
  412.5 6.3 %fusion.3 = f32[16,8,8,128,1,1,1]{3,0,6,4,1,2,5:T(8,128)S(1)} fusion(f32[8,8,128,2,3,3,4]{2,1,0,6,3,5,4:T(8,128)} %reshape.773, f32[3,3,2,4,16]{4,3,2,1,0:T(4,128)S(1)} %reshape.735), kind=kOutput, calls=%fused_computation.83 | convolution fusion | flops 113246208 | bytes 2888192 | tf_op jit(solution)/shard_map/ijanc,ijanb->bc/dot_general | solution.py:142
  418.8 2.1 pad_maximum_fusion
  421.0 2.3 fusion.22
  424.5 11.6 %all-gather.2.cloned.1.call-done = f32[32,8192]{1,0:T(8,128)} async-done(((f32[16,8192]{1,0:T(8,128)}), f32[32,8192]{1,0:T(8,128)}) %all-gather.2.cloned.1.call-update) | async-done | bytes 1048592 | tf_op jit(solution)/shard_map/all_gather | solution.py:169
  436.1 2.4 convolution_multiply_fusion.1
  438.8 40.8 %psum.14 = f32[32,32]{1,0:T(8,128)S(1)} all-reduce(f32[32,32]{1,0:T(8,128)S(1)} %dynamic_update_slice.6), channel_id=1, replica_groups=mesh['gx'=4,'gy'=4,'band'=2] {'gx','gy','band'}, use_global_device_ids=true, to_apply=%region_1.2 | all-reduce | flops 1024 | bytes 8192 | tf_op jit(solution)/shard_map/psum | solution.py:171
  479.7 2.9 cholesky.16
  484.0 2.4 custom-call.6
  486.6 2.2 fusion.191
  489.7 3.0 fusion.162
  492.8 4.2 collective-permute-start.36
  499.8 4.6 collective-permute-start.33
  507.1 4.5 collective-permute-start.38
  512.1 9.6 %collective-permute-done.32 = f32[16,6,8,128]{3,0,2,1:T(8,128)S(1)} collective-permute-done((f32[16,6,8,128]{3,0,2,1:T(8,128)S(1)}, f32[16,6,8,128]{3,0,2,1:T(8,128)S(1)}, u32[]{:S(2)}, u32[]{:S(2)}) %collective-permute-start.32) | collective-permute-done | bytes 393248 | tf_op jit(solution)/shard_map/ppermute | solution.py:31
  524.3 4.3 collective-permute-start.35
  533.2 4.5 collective-permute-start.40
  540.3 5.4 collective-permute-start.42
  545.8 5.0 collective-permute-done.43
  550.9 6.4 %fusion.1 = f32[16,8,8,128,1,1,1]{3,0,6,4,1,2,5:T(8,128)S(1)} fusion(f32[8,8,128,2,3,3,4]{2,1,0,6,3,5,4:T(8,128)} %reshape.773, f32[3,3,2,4,16]{4,3,2,1,0:T(4,128)S(1)} %reshape.740), kind=kOutput, calls=%fused_computation.81 | convolution fusion | flops 113246208 | bytes 2888192 | tf_op jit(solution)/shard_map/ijanc,ijanb->bc/dot_general | solution.py:142
  557.3 3.6 fusion.99
  562.5 38.2 %psum.15 = f32[32,32]{1,0:T(8,128)S(1)} all-reduce(f32[32,32]{1,0:T(8,128)S(1)} %dynamic_update_slice.7), channel_id=1, replica_groups=mesh['gx'=4,'gy'=4,'band'=2] {'gx','gy','band'}, use_global_device_ids=true, to_apply=%region_4.5 | all-reduce | flops 1024 | bytes 8192 | tf_op jit(solution)/shard_map/psum | solution.py:179
  (184 shorter events, 66.0 us)
Async XLA Ops:
  7.2 429.0 %all-gather.2.cloned.1.call-start = ((), (), s32[]{:S(2)}) async-start(), calls=%async_computation | async-start | bytes 1572864 | tf_op jit(solution)/shard_map/all_gather | solution.py:169
  8.7 16.4 %collective-permute-start.5 = (s32[3,1,1,2,512]{4,3,2,1,0:T(2,128)S(1)}, s32[3,1,1,2,512]{4,3,2,1,0:T(2,128)S(1)}, u32[]{:S(2)}, u32[]{:S(2)}) collective-permute-start(s32[3,1,1,2,512]{4,3,2,1,0:T(2,128)S(1)} %pad_add_fusion.2), channel_id=1, source_target_pairs={{8,0},{16,8},{24,16},{9,1},{17,9},{25,17},{10,2},{18,10},{26,18},{... | collective-permute-start | bytes 36872 | tf_op jit(solution)/shard_map/ppermute | solution.py:31
  10.0 15.1 %collective-permute-start.4 = (s32[3,1,1,2,512]{4,3,2,1,0:T(2,128)S(1)}, s32[3,1,1,2,512]{4,3,2,1,0:T(2,128)S(1)}, u32[]{:S(2)}, u32[]{:S(2)}) collective-permute-start(s32[3,1,1,2,512]{4,3,2,1,0:T(2,128)S(1)} %pad_add_fusion.2), channel_id=1, source_target_pairs={{0,8},{8,16},{16,24},{1,9},{9,17},{17,25},{2,10},{10,18},{18,26},{... | collective-permute-start | bytes 36872 | tf_op jit(solution)/shard_map/ppermute | solution.py:29
  15.5 15.5 %collective-permute-start.8 = (f32[1,1,2,4,512]{4,3,2,1,0:T(4,128)}, f32[1,1,2,4,512]{4,3,2,1,0:T(4,128)S(1)}, u32[]{:S(2)}, u32[]{:S(2)}) collective-permute-start(f32[1,1,2,4,512]{4,3,2,1,0:T(4,128)} %param.10), channel_id=1, source_target_pairs={{0,8},{8,16},{16,24},{1,9},{9,17},{17,25},{2,10},{10,18},{18,26},{... | collective-permute-start | bytes 49160 | tf_op jit(solution)/shard_map/ppermute | solution.py:29
  20.3 11.4 %collective-permute-start.9 = (f32[1,1,2,4,512]{4,3,2,1,0:T(4,128)}, f32[1,1,2,4,512]{4,3,2,1,0:T(4,128)S(1)}, u32[]{:S(2)}, u32[]{:S(2)}) collective-permute-start(f32[1,1,2,4,512]{4,3,2,1,0:T(4,128)} %param.10), channel_id=1, source_target_pairs={{8,0},{16,8},{24,16},{9,1},{17,9},{25,17},{10,2},{18,10},{26,18},{... | collective-permute-start | bytes 49160 | tf_op jit(solution)/shard_map/ppermute | solution.py:31
  23.0 259.4 %copy-start.5 = (f32[16,8,8,128]{3,0,2,1:T(8,128)}, f32[16,8,8,128]{3,0,2,1:T(8,128)S(1)}, u32[]{:S(2)}) copy-start(f32[16,8,8,128]{3,0,2,1:T(8,128)S(1)} %copy.89) | copy-start | bytes 1572868
  25.1 12.5 %collective-permute-start.7 = (s32[3,3,1,2,512]{4,3,2,1,0:T(2,128)S(1)}, s32[3,3,1,2,512]{4,3,2,1,0:T(2,128)S(1)}, u32[]{:S(2)}, u32[]{:S(2)}) collective-permute-start(s32[3,3,1,2,512]{4,3,2,1,0:T(2,128)S(1)} %pad_add_fusion.1), channel_id=1, source_target_pairs={{2,0},{4,2},{6,4},{3,1},{5,3},{7,5},{10,8},{12,10},{14,12},{11,9},... | collective-permute-start | bytes 110600 | tf_op jit(solution)/shard_map/ppermute | solution.py:31
  26.4 11.2 %collective-permute-start.6 = (s32[3,3,1,2,512]{4,3,2,1,0:T(2,128)S(1)}, s32[3,3,1,2,512]{4,3,2,1,0:T(2,128)S(1)}, u32[]{:S(2)}, u32[]{:S(2)}) collective-permute-start(s32[3,3,1,2,512]{4,3,2,1,0:T(2,128)S(1)} %pad_add_fusion.1), channel_id=1, source_target_pairs={{0,2},{2,4},{4,6},{1,3},{3,5},{5,7},{8,10},{10,12},{12,14},{9,11},... | collective-permute-start | bytes 110600 | tf_op jit(solution)/shard_map/ppermute | solution.py:29
  31.7 6.6 %collective-permute-start.11 = (f32[3,1,2,4,512]{4,3,2,1,0:T(4,128)S(1)}, f32[3,1,2,4,512]{4,3,2,1,0:T(4,128)S(1)}, u32[]{:S(2)}, u32[]{:S(2)}) collective-permute-start(f32[3,1,2,4,512]{4,3,2,1,0:T(4,128)S(1)} %constant_dynamic-update-slice_fusion.7), channel_id=1, source_target_pairs={{2,0},{4,2},{6,4},{3,1},{5,3},{7,5},{10,8},{12,10},{14,12},{11,9},... | collective-permute-start | bytes 147464 | tf_op jit(solution)/shard_map/ppermute | solution.py:31
  33.0 6.3 %collective-permute-start.10 = (f32[3,1,2,4,512]{4,3,2,1,0:T(4,128)S(1)}, f32[3,1,2,4,512]{4,3,2,1,0:T(4,128)S(1)}, u32[]{:S(2)}, u32[]{:S(2)}) collective-permute-start(f32[3,1,2,4,512]{4,3,2,1,0:T(4,128)S(1)} %constant_dynamic-update-slice_fusion.7), channel_id=1, source_target_pairs={{0,2},{2,4},{4,6},{1,3},{3,5},{5,7},{8,10},{10,12},{12,14},{9,11},... | collective-permute-start | bytes 147464 | tf_op jit(solution)/shard_map/ppermute | solution.py:29
  274.7 33.3 %copy-start.4 = (f32[16,8,8,128]{3,2,1,0:T(8,128)S(1)}, f32[16,8,8,128]{3,2,1,0:T(8,128)}, u32[]{:S(2)}) copy-start(f32[16,8,8,128]{3,2,1,0:T(8,128)} %param.6) | copy-start | bytes 1572868
  278.9 8.4 %collective-permute-start.12 = (f32[1,1,1152]{2,1,0:T(1,128)S(1)}, f32[1,1,1152]{2,1,0:T(1,128)S(1)}, u32[]{:S(2)}, u32[]{:S(2)}) collective-permute-start(f32[1,1,1152]{2,1,0:T(1,128)S(1)} %reshape.729), channel_id=1, source_target_pairs={{0,8},{8,16},{16,24},{1,9},{9,17},{17,25},{2,10},{10,18},{18,26},{... | collective-permute-start | bytes 13832 | tf_op jit(solution)/shard_map/ppermute | solution.py:29
  282.5 24.6 %collective-permute-start.1 = (f32[16,6,8,128]{3,0,2,1:T(8,128)S(1)}, f32[16,6,8,128]{3,0,2,1:T(8,128)S(1)}, u32[]{:S(2)}, u32[]{:S(2)}) collective-permute-start(f32[16,6,8,128]{3,0,2,1:T(8,128)S(1)} %get-tuple-element.27), channel_id=1, source_target_pairs={{0,8},{8,16},{16,24},{1,9},{9,17},{17,25},{2,10},{10,18},{18,26},{... | collective-permute-start | bytes 1179656 | tf_op jit(solution)/shard_map/ppermute | solution.py:29
  284.7 24.6 %collective-permute-start = (f32[16,6,8,128]{3,0,2,1:T(8,128)S(1)}, f32[16,6,8,128]{3,0,2,1:T(8,128)S(1)}, u32[]{:S(2)}, u32[]{:S(2)}) collective-permute-start(f32[16,6,8,128]{3,0,2,1:T(8,128)S(1)} %get-tuple-element.26), channel_id=1, source_target_pairs={{8,0},{16,8},{24,16},{9,1},{17,9},{25,17},{10,2},{18,10},{26,18},{... | collective-permute-start | bytes 1179656 | tf_op jit(solution)/shard_map/ppermute | solution.py:31
  286.0 15.3 %collective-permute-start.13 = (f32[1,1,1152]{2,1,0:T(1,128)S(1)}, f32[1,1,1152]{2,1,0:T(1,128)S(1)}, u32[]{:S(2)}, u32[]{:S(2)}) collective-permute-start(f32[1,1,1152]{2,1,0:T(1,128)S(1)} %reshape.729), channel_id=1, source_target_pairs={{8,0},{16,8},{24,16},{9,1},{17,9},{25,17},{10,2},{18,10},{26,18},{... | collective-permute-start | bytes 13832 | tf_op jit(solution)/shard_map/ppermute | solution.py:31
  301.3 15.8 %collective-permute-start.15 = (f32[3,1,1152]{2,1,0:T(1,128)S(1)}, f32[3,1,1152]{2,1,0:T(1,128)S(1)}, u32[]{:S(2)}, u32[]{:S(2)}) collective-permute-start(f32[3,1,1152]{2,1,0:T(1,128)S(1)} %constant_dynamic-update-slice_fusion.10), channel_id=1, source_target_pairs={{2,0},{4,2},{6,4},{3,1},{5,3},{7,5},{10,8},{12,10},{14,12},{11,9},... | collective-permute-start | bytes 41480 | tf_op jit(solution)/shard_map/ppermute | solution.py:31
  302.6 14.5 %collective-permute-start.14 = (f32[3,1,1152]{2,1,0:T(1,128)S(1)}, f32[3,1,1152]{2,1,0:T(1,128)S(1)}, u32[]{:S(2)}, u32[]{:S(2)}) collective-permute-start(f32[3,1,1152]{2,1,0:T(1,128)S(1)} %constant_dynamic-update-slice_fusion.10), channel_id=1, source_target_pairs={{0,2},{2,4},{4,6},{1,3},{3,5},{5,7},{8,10},{10,12},{12,14},{9,11},... | collective-permute-start | bytes 41480 | tf_op jit(solution)/shard_map/ppermute | solution.py:29
  312.7 36.6 %collective-permute-start.3 = (f32[16,20,6,128]{3,0,2,1:T(8,128)}, f32[16,20,6,128]{3,0,2,1:T(8,128)}, u32[]{:S(2)}, u32[]{:S(2)}) collective-permute-start(f32[16,20,6,128]{3,0,2,1:T(8,128)} %get-tuple-element.15), channel_id=1, source_target_pairs={{0,2},{2,4},{4,6},{1,3},{3,5},{5,7},{8,10},{10,12},{12,14},{9,11},... | collective-permute-start | bytes 2949128 | tf_op jit(solution)/shard_map/ppermute | solution.py:29
  315.6 33.7 %collective-permute-start.2 = (f32[16,20,6,128]{3,0,2,1:T(8,128)}, f32[16,20,6,128]{3,0,2,1:T(8,128)}, u32[]{:S(2)}, u32[]{:S(2)}) collective-permute-start(f32[16,20,6,128]{3,0,2,1:T(8,128)} %get-tuple-element.14), channel_id=1, source_target_pairs={{2,0},{4,2},{6,4},{3,1},{5,3},{7,5},{10,8},{12,10},{14,12},{11,9},... | collective-permute-start | bytes 2949128 | tf_op jit(solution)/shard_map/ppermute | solution.py:31
  317.5 5.9 collective-permute-start.17
  318.8 5.8 collective-permute-start.16
  324.6 18.1 %collective-permute-start.19 = (f32[3,1,128]{2,1,0:T(1,128)S(1)}, f32[3,1,128]{2,1,0:T(1,128)S(1)}, u32[]{:S(2)}, u32[]{:S(2)}) collective-permute-start(f32[3,1,128]{2,1,0:T(1,128)S(1)} %pad_maximum_fusion.14), channel_id=1, source_target_pairs={{2,0},{4,2},{6,4},{3,1},{5,3},{7,5},{10,8},{12,10},{14,12},{11,9},... | collective-permute-start | bytes 4616 | tf_op jit(solution)/shard_map/ppermute | solution.py:31
  325.9 16.8 %collective-permute-start.18 = (f32[3,1,128]{2,1,0:T(1,128)S(1)}, f32[3,1,128]{2,1,0:T(1,128)S(1)}, u32[]{:S(2)}, u32[]{:S(2)}) collective-permute-start(f32[3,1,128]{2,1,0:T(1,128)S(1)} %pad_maximum_fusion.14), channel_id=1, source_target_pairs={{0,2},{2,4},{4,6},{1,3},{3,5},{5,7},{8,10},{10,12},{12,14},{9,11},... | collective-permute-start | bytes 4616 | tf_op jit(solution)/shard_map/ppermute | solution.py:29
  365.8 10.1 %collective-permute-start.24 = (f32[1,1,1152]{2,1,0:T(1,128)S(1)}, f32[1,1,1152]{2,1,0:T(1,128)S(1)}, u32[]{:S(2)}, u32[]{:S(2)}) collective-permute-start(f32[1,1,1152]{2,1,0:T(1,128)S(1)} %reshape.733), channel_id=1, source_target_pairs={{0,8},{8,16},{16,24},{1,9},{9,17},{17,25},{2,10},{10,18},{18,26},{... | collective-permute-start | bytes 13832 | tf_op jit(solution)/shard_map/ppermute | solution.py:29
  368.8 7.2 %collective-permute-start.25 = (f32[1,1,1152]{2,1,0:T(1,128)S(1)}, f32[1,1,1152]{2,1,0:T(1,128)S(1)}, u32[]{:S(2)}, u32[]{:S(2)}) collective-permute-start(f32[1,1,1152]{2,1,0:T(1,128)S(1)} %reshape.733), channel_id=1, source_target_pairs={{8,0},{16,8},{24,16},{9,1},{17,9},{25,17},{10,2},{18,10},{26,18},{... | collective-permute-start | bytes 13832 | tf_op jit(solution)/shard_map/ppermute | solution.py:31
  370.1 11.8 %collective-permute-start.21 = (f32[16,6,8,128]{3,0,2,1:T(8,128)S(1)}, f32[16,6,8,128]{3,0,2,1:T(8,128)S(1)}, u32[]{:S(2)}, u32[]{:S(2)}) collective-permute-start(f32[16,6,8,128]{3,0,2,1:T(8,128)S(1)} %get-tuple-element.22), channel_id=1, source_target_pairs={{0,8},{8,16},{16,24},{1,9},{9,17},{17,25},{2,10},{10,18},{18,26},{... | collective-permute-start | bytes 1179656 | tf_op jit(solution)/shard_map/ppermute | solution.py:29
  374.7 13.1 %collective-permute-start.20 = (f32[16,6,8,128]{3,0,2,1:T(8,128)S(1)}, f32[16,6,8,128]{3,0,2,1:T(8,128)S(1)}, u32[]{:S(2)}, u32[]{:S(2)}) collective-permute-start(f32[16,6,8,128]{3,0,2,1:T(8,128)S(1)} %get-tuple-element.21), channel_id=1, source_target_pairs={{8,0},{16,8},{24,16},{9,1},{17,9},{25,17},{10,2},{18,10},{26,18},{... | collective-permute-start | bytes 1179656 | tf_op jit(solution)/shard_map/ppermute | solution.py:31
  376.0 20.2 %collective-permute-start.27 = (f32[3,1,1152]{2,1,0:T(1,128)S(1)}, f32[3,1,1152]{2,1,0:T(1,128)S(1)}, u32[]{:S(2)}, u32[]{:S(2)}) collective-permute-start(f32[3,1,1152]{2,1,0:T(1,128)S(1)} %constant_dynamic-update-slice_fusion.13), channel_id=1, source_target_pairs={{2,0},{4,2},{6,4},{3,1},{5,3},{7,5},{10,8},{12,10},{14,12},{11,9},... | collective-permute-start | bytes 41480 | tf_op jit(solution)/shard_map/ppermute | solution.py:31
  377.3 18.9 %collective-permute-start.26 = (f32[3,1,1152]{2,1,0:T(1,128)S(1)}, f32[3,1,1152]{2,1,0:T(1,128)S(1)}, u32[]{:S(2)}, u32[]{:S(2)}) collective-permute-start(f32[3,1,1152]{2,1,0:T(1,128)S(1)} %constant_dynamic-update-slice_fusion.13), channel_id=1, source_target_pairs={{0,2},{2,4},{4,6},{1,3},{3,5},{5,7},{8,10},{10,12},{12,14},{9,11},... | collective-permute-start | bytes 41480 | tf_op jit(solution)/shard_map/ppermute | solution.py:29
  389.4 29.4 %collective-permute-start.22 = (f32[16,20,6,128]{3,0,2,1:T(8,128)}, f32[16,20,6,128]{3,0,2,1:T(8,128)}, u32[]{:S(2)}, u32[]{:S(2)}) collective-permute-start(f32[16,20,6,128]{3,0,2,1:T(8,128)} %get-tuple-element.12), channel_id=1, source_target_pairs={{2,0},{4,2},{6,4},{3,1},{5,3},{7,5},{10,8},{12,10},{14,12},{11,9},... | collective-permute-start | bytes 2949128 | tf_op jit(solution)/shard_map/ppermute | solution.py:31
  390.7 28.1 %collective-permute-start.23 = (f32[16,20,6,128]{3,0,2,1:T(8,128)}, f32[16,20,6,128]{3,0,2,1:T(8,128)}, u32[]{:S(2)}, u32[]{:S(2)}) collective-permute-start(f32[16,20,6,128]{3,0,2,1:T(8,128)} %get-tuple-element.13), channel_id=1, source_target_pairs={{0,2},{2,4},{4,6},{1,3},{3,5},{5,7},{8,10},{10,12},{12,14},{9,11},... | collective-permute-start | bytes 2949128 | tf_op jit(solution)/shard_map/ppermute | solution.py:29
  398.1 5.9 collective-permute-start.29
  399.3 5.8 collective-permute-start.28
  405.2 6.0 collective-permute-start.31
  406.5 5.8 collective-permute-start.30
  492.8 12.9 %collective-permute-start.36 = (f32[1,1,1152]{2,1,0:T(1,128)S(1)}, f32[1,1,1152]{2,1,0:T(1,128)S(1)}, u32[]{:S(2)}, u32[]{:S(2)}) collective-permute-start(f32[1,1,1152]{2,1,0:T(1,128)S(1)} %reshape.738), channel_id=1, source_target_pairs={{0,8},{8,16},{16,24},{1,9},{9,17},{17,25},{2,10},{10,18},{18,26},{... | collective-permute-start | bytes 13832 | tf_op jit(solution)/shard_map/ppermute | solution.py:29
  497.0 8.8 %collective-permute-start.37 = (f32[1,1,1152]{2,1,0:T(1,128)S(1)}, f32[1,1,1152]{2,1,0:T(1,128)S(1)}, u32[]{:S(2)}, u32[]{:S(2)}) collective-permute-start(f32[1,1,1152]{2,1,0:T(1,128)S(1)} %reshape.738), channel_id=1, source_target_pairs={{8,0},{16,8},{24,16},{9,1},{17,9},{25,17},{10,2},{18,10},{26,18},{... | collective-permute-start | bytes 13832 | tf_op jit(solution)/shard_map/ppermute | solution.py:31
  499.4 12.6 %copy-start.6 = (f32[2,8,64,128]{3,2,1,0:T(8,128)}, f32[2,8,64,128]{3,2,1,0:T(8,128)S(1)}, u32[]{:S(2)}) copy-start(f32[2,8,64,128]{3,2,1,0:T(8,128)S(1)} %copy.151) | copy-start | bytes 1572868
  499.8 11.8 %collective-permute-start.33 = (f32[16,6,8,128]{3,0,2,1:T(8,128)S(1)}, f32[16,6,8,128]{3,0,2,1:T(8,128)S(1)}, u32[]{:S(2)}, u32[]{:S(2)}) collective-permute-start(f32[16,6,8,128]{3,0,2,1:T(8,128)S(1)} %get-tuple-element.20), channel_id=1, source_target_pairs={{0,8},{8,16},{16,24},{1,9},{9,17},{17,25},{2,10},{10,18},{18,26},{... | collective-permute-start | bytes 1179656 | tf_op jit(solution)/shard_map/ppermute | solution.py:29
  504.4 17.3 %collective-permute-start.32 = (f32[16,6,8,128]{3,0,2,1:T(8,128)S(1)}, f32[16,6,8,128]{3,0,2,1:T(8,128)S(1)}, u32[]{:S(2)}, u32[]{:S(2)}) collective-permute-start(f32[16,6,8,128]{3,0,2,1:T(8,128)S(1)} %get-tuple-element.19), channel_id=1, source_target_pairs={{8,0},{16,8},{24,16},{9,1},{17,9},{25,17},{10,2},{18,10},{26,18},{... | collective-permute-start | bytes 1179656 | tf_op jit(solution)/shard_map/ppermute | solution.py:31
  505.8 24.2 %collective-permute-start.39 = (f32[3,1,1152]{2,1,0:T(1,128)S(1)}, f32[3,1,1152]{2,1,0:T(1,128)S(1)}, u32[]{:S(2)}, u32[]{:S(2)}) collective-permute-start(f32[3,1,1152]{2,1,0:T(1,128)S(1)} %constant_dynamic-update-slice_fusion.23), channel_id=1, source_target_pairs={{2,0},{4,2},{6,4},{3,1},{5,3},{7,5},{10,8},{12,10},{14,12},{11,9},... | collective-permute-start | bytes 41480 | tf_op jit(solution)/shard_map/ppermute | solution.py:31
  507.1 22.9 %collective-permute-start.38 = (f32[3,1,1152]{2,1,0:T(1,128)S(1)}, f32[3,1,1152]{2,1,0:T(1,128)S(1)}, u32[]{:S(2)}, u32[]{:S(2)}) collective-permute-start(f32[3,1,1152]{2,1,0:T(1,128)S(1)} %constant_dynamic-update-slice_fusion.23), channel_id=1, source_target_pairs={{0,2},{2,4},{4,6},{1,3},{3,5},{5,7},{8,10},{10,12},{12,14},{9,11},... | collective-permute-start | bytes 41480 | tf_op jit(solution)/shard_map/ppermute | solution.py:29
  524.3 33.0 %collective-permute-start.35 = (f32[16,20,6,128]{3,0,2,1:T(8,128)}, f32[16,20,6,128]{3,0,2,1:T(8,128)}, u32[]{:S(2)}, u32[]{:S(2)}) collective-permute-start(f32[16,20,6,128]{3,0,2,1:T(8,128)} %get-tuple-element.9), channel_id=1, source_target_pairs={{0,2},{2,4},{4,6},{1,3},{3,5},{5,7},{8,10},{10,12},{12,14},{9,11},... | collective-permute-start | bytes 2949128 | tf_op jit(solution)/shard_map/ppermute | solution.py:29
  528.6 28.6 %collective-permute-start.34 = (f32[16,20,6,128]{3,0,2,1:T(8,128)}, f32[16,20,6,128]{3,0,2,1:T(8,128)}, u32[]{:S(2)}, u32[]{:S(2)}) collective-permute-start(f32[16,20,6,128]{3,0,2,1:T(8,128)} %get-tuple-element.8), channel_id=1, source_target_pairs={{2,0},{4,2},{6,4},{3,1},{5,3},{7,5},{10,8},{12,10},{14,12},{11,9},... | collective-permute-start | bytes 2949128 | tf_op jit(solution)/shard_map/ppermute | solution.py:31
  531.9 5.9 collective-permute-start.41
  533.2 5.8 collective-permute-start.40
  539.1 11.7 %collective-permute-start.43 = (f32[3,1,128]{2,1,0:T(1,128)S(1)}, f32[3,1,128]{2,1,0:T(1,128)S(1)}, u32[]{:S(2)}, u32[]{:S(2)}) collective-permute-start(f32[3,1,128]{2,1,0:T(1,128)S(1)} %pad_maximum_fusion.16), channel_id=1, source_target_pairs={{2,0},{4,2},{6,4},{3,1},{5,3},{7,5},{10,8},{12,10},{14,12},{11,9},... | collective-permute-start | bytes 4616 | tf_op jit(solution)/shard_map/ppermute | solution.py:31
  540.3 10.4 %collective-permute-start.42 = (f32[3,1,128]{2,1,0:T(1,128)S(1)}, f32[3,1,128]{2,1,0:T(1,128)S(1)}, u32[]{:S(2)}, u32[]{:S(2)}) collective-permute-start(f32[3,1,128]{2,1,0:T(1,128)S(1)} %pad_maximum_fusion.16), channel_id=1, source_target_pairs={{0,2},{2,4},{4,6},{1,3},{3,5},{5,7},{8,10},{10,12},{12,14},{9,11},... | collective-permute-start | bytes 4616 | tf_op jit(solution)/shard_map/ppermute | solution.py:29
  (12 other events, 57.3 us)
Sparse Core Ops, SparseCore 0:
  424.6 11.4 all-gather.1
where the time goes:
time: 617 us; the launch traced here: 610 us
  other arithmetic  261 us (42%)
  starting transfers between devices  132 us (21%)
  blocking collectives  79.1 us (13%)
  waiting for transfers between devices  54.4 us (9%)
  matrix products  37.1 us (6%)
  local copies, waits for them, and re-layouts  31.6 us (5%)
  between operations  15.4 us (2%)
    scatter-add x1, other arithmetic, prepare_tables(): table_near = jnp.zeros((9 * atom_count * proj_count * cell_count,), jnp.f...  233 us
    ppermute x22, starting transfers between devices, with_halo(): lax.ppermute(tail, axis, [(i, (i + 1) % count) for i in range(ends)])  103 us
    psum x1, blocking collectives, per_device(): lax.psum(lax.dynamic_update_slice(empty_square, over_cols, (0, band_start...  40.8 us
    psum x1, blocking collectives, per_device(): lax.psum(lax.dynamic_update_slice(empty_square, sub_cols, (0, band_start)...  38.2 us
    ppermute x22, waiting for transfers between devices, with_halo(): lax.ppermute(head, axis, [((i + 1) % count, i) for i in range(ends)])  36.9 us
    ppermute x22, starting transfers between devices, with_halo(): lax.ppermute(head, axis, [((i + 1) % count, i) for i in range(ends)])  28.3 us
    dot_general x3, matrix products, apply_hamiltonian(): jnp.einsum('ijanc,ijanb->bc', table_near, near_coefs, precision=highest)  19.1 us
  transfers between devices with their start and end apart: 45, of which 11 were waited for; matrix products, arithmetic and copies ran while one was open for 7% of the time, Pallas kernels for 0%

commit v1 on v0

--- a/solution.py
+++ b/solution.py
@@ -1,6 +1,11 @@
+import functools
+
 import jax
 import jax.numpy as jnp
+import numpy as np
 from jax import lax
+from jax.experimental import pallas as pl
+from jax.experimental.pallas import tpu as pltpu
 from jax.sharding import PartitionSpec as P
 
 spacing = 0.4
@@ -149,7 +154,7 @@
     return lax.linalg.triangular_solve(factor, identity, left_side=True, lower=True)
 
 
-def per_device(orbitals, local_potential, atom_cell, support_offset, projector, coupling):
+def per_device_halo(orbitals, local_potential, atom_cell, support_offset, projector, coupling):
     orb_count, size_x, size_y, size_z = orbitals.shape
     tables = prepare_tables(atom_cell, support_offset, projector, size_x, size_y, size_z)
     coupling_own = coupling[0, 0]
@@ -186,6 +191,520 @@
     return (rotated.reshape(orbitals.shape), residual.reshape(orbitals.shape), subspace)
 
 
+MESH = pl.DeviceIdType.MESH
+reach = 6
+box = 2 * reach + 1
+box_y = 16
+pad_y = 8
+scale = -0.5 / spacing**2
+
+
+def gather_kernel(dims, orb_ref, pot_ref, pack_ref, orb_out, pot_out, pack_out, local_sem, send_sem, recv_sem):
+    dom_x, dom_y = dims
+    count = dom_x * dom_y
+    my_x, my_y = lax.axis_index("gx"), lax.axis_index("gy")
+    me = my_x * dom_y + my_y
+
+    barrier = pltpu.get_barrier_semaphore()
+
+    def greet(step, carry):
+        peer = lax.rem(me + step, count)
+        pl.semaphore_signal(
+            barrier, inc=1, device_id={"gx": peer // dom_y, "gy": lax.rem(peer, dom_y)}, device_id_type=MESH
+        )
+        return carry
+
+    def parts(peer, source_x, source_y):
+        source = source_x * dom_y + source_y
+        target = {"gx": peer // dom_y, "gy": lax.rem(peer, dom_y)}
+        pairs = (
+            (pack_ref, pack_out.at[source]),
+            (pot_ref, pot_out.at[source_x, :, source_y]),
+            (orb_ref.at[peer], orb_out.at[source_x, :, source_y]),
+        )
+        return [
+            pltpu.make_async_remote_copy(
+                src_ref=src,
+                dst_ref=dst,
+                send_sem=send_sem.at[kind, peer],
+                recv_sem=recv_sem.at[kind, source],
+                device_id=target,
+                device_id_type=MESH,
+            )
+            for kind, (src, dst) in enumerate(pairs)
+        ]
+
+    lax.fori_loop(1, count, greet, 0)
+    own = [
+        pltpu.make_async_copy(pack_ref, pack_out.at[me], local_sem.at[0]),
+        pltpu.make_async_copy(pot_ref, pot_out.at[my_x, :, my_y], local_sem.at[1]),
+        pltpu.make_async_copy(orb_ref.at[me], orb_out.at[my_x, :, my_y], local_sem.at[2]),
+    ]
+    for copy in own:
+        copy.start()
+    pl.semaphore_wait(barrier, count - 1)
+
+    def send(step, carry):
+        for copy in parts(lax.rem(me + step, count), my_x, my_y):
+            copy.start()
+        return carry
+
+    def finish(step, carry):
+        peer = lax.rem(me + step, count)
+        for copy in parts(peer, my_x, my_y):
+            copy.wait_send()
+        for copy in parts(peer, peer // dom_y, lax.rem(peer, dom_y)):
+            copy.wait_recv()
+        return carry
+
+    lax.fori_loop(1, count, send, 0)
+    lax.fori_loop(1, count, finish, 0)
+    for copy in own:
+        copy.wait()
+
+
+def compute_kernel(
+    dims, home_ref, orb_ref, pot_ref, pack_ref, coup_ref, along_ref, filt_out, image_out, table, field, out, sums, coefs
+):
+    count, atom_count, proj_count = dims
+    nx, ny, nz = orb_ref.shape
+    points = pack_ref.shape[2]
+    rows = box * box_y
+    wide = 16
+    lane = lax.broadcasted_iota(jnp.int32, (rows, nz), 1)
+    row_xy = lax.broadcasted_iota(jnp.int32, (rows, points), 0)
+    row_z = lax.broadcasted_iota(jnp.int32, (wide, points), 0)
+
+    def build(dom, carry):
+        for atom in range(atom_count):
+            cell = pack_ref[dom, 8 + atom : 9 + atom, :].astype(jnp.int32)
+            hot_xy = jnp.where(row_xy == lax.shift_right_arithmetic(cell, 4), 1.0, 0.0).astype(jnp.bfloat16)
+            hot_z = row_z == (cell & 15)
+            values = jnp.concatenate(
+                [
+                    jnp.where(hot_z, pack_ref[dom, proj_count * atom + n : proj_count * atom + n + 1, :], 0.0)
+                    for n in range(proj_count)
+                ],
+                axis=0,
+            )
+            high = values.astype(jnp.bfloat16)
+            low = (values - high.astype(jnp.float32)).astype(jnp.bfloat16)
+            both = jnp.concatenate([high, low], axis=0)
+            boxes = lax.dot_general(hot_xy, both, (((1,), (1,)), ((), ())), preferred_element_type=jnp.float32)
+            boxes = boxes + pltpu.roll(boxes, proj_count * wide, 1)
+            at = dom * atom_count + atom
+            low_z = home_ref[2, at] - reach
+            for n in range(proj_count):
+                kept = jnp.where((lane >= n * wide) & (lane < (n + 1) * wide), boxes, 0.0)
+                moved = pltpu.roll(kept, lax.rem(low_z - n * wide + 2 * nz, nz), 1)
+                table[at, n] = moved.reshape(box, box_y, nz)
+        return carry
+
+    field[...] = jnp.zeros_like(field)
+    out[...] = jnp.zeros_like(out)
+    inner = pl.ds(pad_y, ny)
+    field[reach : reach + nx, pad_y : pad_y + ny, :] = orb_ref[...]
+    lax.fori_loop(0, count, build, 0)
+
+    def hamiltonian():
+        def project(at, carry):
+            x0, y0 = home_ref[0, at], home_ref[1, at]
+            totals = [jnp.zeros((box_y, nz), jnp.float32) for _ in range(proj_count)]
+            for dx in range(box):
+                part = field[x0 + dx, pl.ds(y0, box_y), :]
+                for n in range(proj_count):
+                    totals[n] = totals[n] + table[at, n, dx] * part
+            stacked = [jnp.sum(total, axis=0, keepdims=True) for total in totals]
+            sums[at] = jnp.concatenate(stacked, axis=0)
+            return carry
+
+        lax.fori_loop(0, count * atom_count, project, 0)
+        scaled = jnp.sum(sums[...], axis=2, keepdims=True) * coup_ref[...]
+        coefs[...] = jnp.broadcast_to(scaled, coefs.shape)
+
+        chunk = 8
+        for start in range(0, nx, chunk):
+            block = field[reach + start : reach + start + chunk, pad_y : pad_y + ny, :]
+            z_part = jnp.dot(
+                block.reshape(chunk * ny, nz), along_ref[...], precision=highest, preferred_element_type=jnp.float32
+            )
+            out[reach + start : reach + start + chunk, pad_y : pad_y + ny, :] = z_part.reshape(chunk, ny, nz)
+
+        def stencil_row(row, carry):
+            at = row + reach
+            summed = out[at, inner, :] + pot_ref[row] * field[at, inner, :]
+            for k in range(1, reach + 1):
+                around = (
+                    field[at + k, inner, :]
+                    + field[at - k, inner, :]
+                    + field[at, pl.ds(pad_y + k, ny), :]
+                    + field[at, pl.ds(pad_y - k, ny), :]
+                )
+                summed = summed + (scale * stencil[k]) * around
+            out[at, inner, :] = summed
+            return carry
+
+        lax.fori_loop(0, nx, stencil_row, 0)
+
+        def spread(at, carry):
+            x0, y0 = home_ref[0, at], home_ref[1, at]
+            weights = [jnp.broadcast_to(coefs[at, n : n + 1, :], (box_y, nz)) for n in range(proj_count)]
+            for dx in range(box):
+                added = out[x0 + dx, pl.ds(y0, box_y), :]
+                for n in range(proj_count):
+                    added = added + table[at, n, dx] * weights[n]
+                out[x0 + dx, pl.ds(y0, box_y), :] = added
+            return carry
+
+        lax.fori_loop(0, count * atom_count, spread, 0)
+
+    middle = 0.5 * (top_edge + low_edge)
+    half_width = 0.5 * (top_edge - low_edge)
+    hamiltonian()
+
+    def first_row(row, carry):
+        at = row + reach
+        field[at, inner, :] = (out[at, inner, :] - middle * field[at, inner, :]) * (1.0 / half_width)
+        return carry
+
+    lax.fori_loop(0, nx, first_row, 0)
+    hamiltonian()
+
+    def filter_row(row, carry):
+        at = row + reach
+        value = (out[at, inner, :] - middle * field[at, inner, :]) * (2.0 / half_width) - orb_ref[row]
+        field[at, inner, :] = value
+        filt_out[row] = value
+        return carry
+
+    lax.fori_loop(0, nx, filter_row, 0)
+    hamiltonian()
+    image_out[...] = out[reach : reach + nx, pad_y : pad_y + ny, :]
+
+
+def project_kernel(
+    dims,
+    filt_ref,
+    image_ref,
+    new_out,
+    res_out,
+    sub_out,
+    cells,
+    result,
+    plane,
+    column,
+    local_sem,
+    send_sem,
+    recv_sem,
+    plane_send,
+    plane_recv,
+    column_send,
+    column_recv,
+    out_sem,
+    pair_send,
+    pair_recv,
+):
+    dom_x, dom_y, bands, total_cells = dims
+    per_band = dom_x * dom_y
+    orbs = per_band * bands
+    my_x, my_y, my_band = lax.axis_index("gx"), lax.axis_index("gy"), lax.axis_index("band")
+    me = my_band * per_band + my_x * dom_y + my_y
+    rows = cells.shape[1] * cells.shape[2]
+
+    def place(peer):
+        inside = lax.rem(peer, per_band)
+        return {"gx": inside // dom_y, "gy": lax.rem(inside, dom_y), "band": peer // per_band}
+
+    barrier = pltpu.get_barrier_semaphore()
+
+    def greet(step, carry):
+        pl.semaphore_signal(barrier, inc=1, device_id=place(lax.rem(me + step, orbs)), device_id_type=MESH)
+        return carry
+
+    lax.fori_loop(1, orbs, greet, 0)
+
+    def chunk_of(ref, peer):
+        inside = lax.rem(peer, per_band)
+        return ref.at[inside // dom_y, peer // per_band, :, lax.rem(inside, dom_y)]
+
+    def parts(peer, source):
+        return [
+            pltpu.make_async_remote_copy(
+                src_ref=chunk_of(ref, peer),
+                dst_ref=cells.at[kind * orbs + source],
+                send_sem=send_sem.at[kind, peer],
+                recv_sem=recv_sem.at[kind, source],
+                device_id=place(peer),
+                device_id_type=MESH,
+            )
+            for kind, ref in enumerate((filt_ref, image_ref))
+        ]
+
+    own = [
+        pltpu.make_async_copy(chunk_of(ref, me), cells.at[kind * orbs + me], local_sem.at[kind])
+        for kind, ref in enumerate((filt_ref, image_ref))
+    ]
+    for copy in own:
+        copy.start()
+    pl.semaphore_wait(barrier, orbs - 1)
+
+    def send(step, carry):
+        for copy in parts(lax.rem(me + step, orbs), me):
+            copy.start()
+        return carry
+
+    def finish(step, carry):
+        peer = lax.rem(me + step, orbs)
+        for copy in parts(peer, me):
+            copy.wait_send()
+        for copy in parts(peer, peer):
+            copy.wait_recv()
+        return carry
+
+    lax.fori_loop(1, orbs, send, 0)
+    lax.fori_loop(1, orbs, finish, 0)
+    for copy in own:
+        copy.wait()
+
+    flat = cells.reshape(2 * orbs * rows, cells.shape[3])
+    gram = jnp.zeros((orbs, 2 * orbs), jnp.float32)
+    for row in range(rows):
+        both = flat[pl.ds(row, 2 * orbs, stride=rows), :]
+        gram = gram + lax.dot_general(
+            both[:orbs],
+            both,
+            (((1,), (1,)), ((), ())),
+            precision=highest,
+            preferred_element_type=jnp.float32,
+        )
+
+    in_plane = dom_x * bands
+    my_plane = my_x * bands + my_band
+    plane[my_plane] = gram
+
+    def plane_copy(peer, slot):
+        return pltpu.make_async_remote_copy(
+            src_ref=plane.at[my_plane],
+            dst_ref=plane.at[slot],
+            send_sem=plane_send.at[peer],
+            recv_sem=plane_recv.at[slot],
+            device_id={"gx": peer // bands, "gy": my_y, "band": lax.rem(peer, bands)},
+            device_id_type=MESH,
+        )
+
+    for step in range(1, in_plane):
+        plane_copy(lax.rem(my_plane + step, in_plane), my_plane).start()
+    for step in range(1, in_plane):
+        peer = lax.rem(my_plane + step, in_plane)
+        plane_copy(peer, my_plane).wait_send()
+        plane_copy(peer, peer).wait_recv()
+    total = plane[0]
+    for slot in range(1, in_plane):
+        total = total + plane[slot]
+    column[my_y] = total
+
+    def column_copy(peer, slot):
+        return pltpu.make_async_remote_copy(
+            src_ref=column.at[my_y],
+            dst_ref=column.at[slot],
+            send_sem=column_send.at[peer],
+            recv_sem=column_recv.at[slot],
+            device_id={"gx": my_x, "gy": peer, "band": my_band},
+            device_id_type=MESH,
+        )
+
+    for step in range(1, dom_y):
+        column_copy(lax.rem(my_y + step, dom_y), my_y).start()
+    for step in range(1, dom_y):
+        peer = lax.rem(my_y + step, dom_y)
+        column_copy(peer, my_y).wait_send()
+        column_copy(peer, peer).wait_recv()
+    total = column[0]
+    for slot in range(1, dom_y):
+        total = total + column[slot]
+    total = total * (1.0 / total_cells)
+
+    row_at = lax.broadcasted_iota(jnp.int32, (orbs, orbs), 0)
+    col_at = lax.broadcasted_iota(jnp.int32, (orbs, orbs), 1)
+    eye = jnp.where(row_at == col_at, 1.0, 0.0)
+    work = jnp.concatenate([total[:, :orbs], eye], axis=1)
+    row_wide = lax.broadcasted_iota(jnp.int32, (orbs, 2 * orbs), 0)
+    for k in range(orbs):
+        pivot_row = work[k : k + 1, :]
+        pivot = work[k : k + 1, k : k + 1]
+        factor = jnp.where(row_wide[:, :1] > k, work[:, k : k + 1] / pivot, 0.0)
+        work = work - factor * pivot_row
+    diagonal = jnp.sum(work[:, :orbs] * eye, axis=1, keepdims=True)
+    inverse = work[:, orbs:] / jnp.sqrt(diagonal)
+
+    def product(left, right, dims_in):
+        return lax.dot_general(left, right, (dims_in, ((), ())), precision=highest, preferred_element_type=jnp.float32)
+
+    projected = product(inverse, total[:, orbs:], ((1,), (0,)))
+    subspace = product(projected, inverse, ((1,), (1,)))
+    sub_out[...] = subspace
+    half_width = 0.5 * (top_edge - low_edge)
+    mixed = product(subspace, inverse, ((0,), (0,))) * (-1.0 / half_width)
+    top = jnp.concatenate([inverse, jnp.zeros_like(inverse)], axis=1)
+    bottom = jnp.concatenate([mixed, inverse * (1.0 / half_width)], axis=1)
+    rotation = jnp.concatenate([top, bottom], axis=0)
+    flat_result = result.reshape(2 * orbs * rows, cells.shape[3])
+    for row in range(rows):
+        both = flat[pl.ds(row, 2 * orbs, stride=rows), :]
+        flat_result[pl.ds(row, 2 * orbs, stride=rows), :] = product(rotation, both, ((1,), (0,)))
+
+    outs = (new_out, res_out)
+    keep = [
+        pltpu.make_async_copy(
+            result.at[pl.ds(kind * orbs + my_band * per_band, per_band)], out.at[:, my_band], out_sem.at[kind]
+        )
+        for kind, out in enumerate(outs)
+    ]
+    for copy in keep:
+        copy.start()
+
+    def pair_copy(kind, other, half):
+        return pltpu.make_async_remote_copy(
+            src_ref=result.at[pl.ds(kind * orbs + other * per_band, per_band)],
+            dst_ref=outs[kind].at[:, half],
+            send_sem=pair_send.at[kind, other],
+            recv_sem=pair_recv.at[kind, half],
+            device_id={"gx": my_x, "gy": my_y, "band": other},
+            device_id_type=MESH,
+        )
+
+    for step in range(1, bands):
+        other = lax.rem(my_band + step, bands)
+        for kind in range(2):
+            pair_copy(kind, other, my_band).start()
+    for step in range(1, bands):
+        other = lax.rem(my_band + step, bands)
+        for kind in range(2):
+            pair_copy(kind, other, my_band).wait_send()
+            pair_copy(kind, other, other).wait_recv()
+    for copy in keep:
+        copy.wait()
+
+
+def per_device_whole(orbitals, local_potential, atom_cell, support_offset, projector, coupling):
+    orb_count, size_x, size_y, nz = orbitals.shape
+    dom_x, dom_y, bands = lax.axis_size("gx"), lax.axis_size("gy"), lax.axis_size("band")
+    count = dom_x * dom_y
+    nx, ny = dom_x * size_x, dom_y * size_y
+    atom_count, proj_count, points = projector.shape[2:]
+    atoms = count * atom_count
+    any_spec = pl.BlockSpec(memory_space=pl.ANY)
+    vmem = pl.BlockSpec(memory_space=pltpu.VMEM)
+    smem = pl.BlockSpec(memory_space=pltpu.SMEM)
+
+    cell = atom_cell[0, 0]
+    offset = support_offset[:, 0, 0]
+    home_z = cell % nz
+    point_z = home_z[:, None] + offset[2]
+    box_cell = ((offset[0] + reach) * box_y + offset[1] + reach) * 16 + offset[2] + reach
+    box_cell = jnp.where((point_z >= 0) & (point_z < nz), box_cell, -1).astype(jnp.float32)
+    small = jnp.concatenate([coupling[0, 0].reshape(-1), cell.astype(jnp.float32)])
+    pack = jnp.concatenate(
+        [
+            projector[0, 0].reshape(atom_count * proj_count, points),
+            box_cell,
+            jnp.pad(small, (0, points - small.shape[0]))[None],
+            jnp.zeros((16 - atom_count * proj_count - atom_count - 1, points), jnp.float32),
+        ],
+        axis=0,
+    )
+    f32 = jnp.float32
+    whole_orb, whole_pot, packs = pl.pallas_call(
+        functools.partial(gather_kernel, (dom_x, dom_y)),
+        out_shape=(
+            jax.ShapeDtypeStruct((dom_x, size_x, dom_y, size_y, nz), f32),
+            jax.ShapeDtypeStruct((dom_x, size_x, dom_y, size_y, nz), f32),
+            jax.ShapeDtypeStruct((count, 16, points), f32),
+        ),
+        in_specs=[any_spec] * 3,
+        out_specs=(any_spec,) * 3,
+        scratch_shapes=[
+            pltpu.SemaphoreType.DMA((3,)),
+            pltpu.SemaphoreType.DMA((3, count)),
+            pltpu.SemaphoreType.DMA((3, count)),
+        ],
+        compiler_params=pltpu.CompilerParams(collective_id=0, has_side_effects=True),
+    )(orbitals, local_potential, pack)
+
+    smalls = packs[:, atom_count * proj_count + atom_count, :]
+    coups = smalls[:, : atom_count * proj_count].reshape(atoms, proj_count, 1)
+    homes = smalls[:, atom_count * proj_count : atom_count * proj_count + atom_count].astype(jnp.int32)
+    dom = jnp.arange(count, dtype=jnp.int32)[:, None]
+    home_x = dom // dom_y * size_x + homes // (size_y * nz)
+    home_y = dom % dom_y * size_y + homes // nz % size_y + pad_y - reach
+    home = jnp.stack([home_x.reshape(-1), home_y.reshape(-1), (homes % nz).reshape(-1)])
+    along = np.zeros((nz, nz), np.float32)
+    for i in range(nz):
+        for j in range(max(0, i - reach), min(nz, i + reach + 1)):
+            along[i, j] = scale * stencil[abs(i - j)] * (3.0 if i == j else 1.0)
+
+    field_shape = (nx + 2 * reach, ny + 2 * pad_y + 8, nz)
+    filt, image = pl.pallas_call(
+        functools.partial(compute_kernel, (count, atom_count, proj_count)),
+        out_shape=(jax.ShapeDtypeStruct((nx, ny, nz), f32),) * 2,
+        in_specs=[smem] + [vmem] * 5,
+        out_specs=(vmem, vmem),
+        scratch_shapes=[
+            pltpu.VMEM((atoms, proj_count, box, box_y, nz), f32),
+            pltpu.VMEM(field_shape, f32),
+            pltpu.VMEM(field_shape, f32),
+            pltpu.VMEM((atoms, proj_count, nz), f32),
+            pltpu.VMEM((atoms, proj_count, nz), f32),
+        ],
+        compiler_params=pltpu.CompilerParams(vmem_limit_bytes=48 << 20),
+    )(home, whole_orb.reshape(nx, ny, nz), whole_pot.reshape(nx, ny, nz), packs, coups, jnp.asarray(along))
+
+    orbs = orb_count * bands
+    half = size_x // bands
+    rows = half * size_y
+    shape = (dom_x, bands, half, dom_y, size_y, nz)
+    sem = pltpu.SemaphoreType.DMA
+    new, res, sub = pl.pallas_call(
+        functools.partial(project_kernel, (dom_x, dom_y, bands, float(nx * ny * nz))),
+        out_shape=(
+            jax.ShapeDtypeStruct((orb_count, bands, half, size_y, nz), f32),
+            jax.ShapeDtypeStruct((orb_count, bands, half, size_y, nz), f32),
+            jax.ShapeDtypeStruct((orbs, orbs), f32),
+        ),
+        in_specs=[any_spec] * 2,
+        out_specs=(any_spec, any_spec, vmem),
+        scratch_shapes=[
+            pltpu.VMEM((2 * orbs, half, size_y, nz), f32),
+            pltpu.VMEM((2 * orbs, half, size_y, nz), f32),
+            pltpu.VMEM((dom_x * bands, orbs, 2 * orbs), f32),
+            pltpu.VMEM((dom_y, orbs, 2 * orbs), f32),
+            sem((2,)),
+            sem((2, orbs)),
+            sem((2, orbs)),
+            sem((dom_x * bands,)),
+            sem((dom_x * bands,)),
+            sem((dom_y,)),
+            sem((dom_y,)),
+            sem((2,)),
+            sem((2, bands)),
+            sem((2, bands)),
+        ],
+        compiler_params=pltpu.CompilerParams(
+            collective_id=1, has_side_effects=True, vmem_limit_bytes=32 << 20
+        ),
+    )(filt.reshape(shape), image.reshape(shape))
+    return (new.reshape(orbitals.shape), res.reshape(orbitals.shape), sub)
+
+
+def per_device(orbitals, local_potential, atom_cell, support_offset, projector, coupling):
+    domains = lax.axis_size("gx") * lax.axis_size("gy")
+    if orbitals.shape[0] == domains and orbitals.shape[1] % lax.axis_size("band") == 0:
+        plan = per_device_whole
+    else:
+        plan = per_device_halo
+    return plan(orbitals, local_potential, atom_cell, support_offset, projector, coupling)
+
+
 def solution(mesh):
     in_specs = (
         P("band", "gx", "gy", None),

time: 617 us -> 125 us (0.20); the launches traced: 610 us -> 125 us
  other arithmetic: 261 us -> 1.12 us
  starting transfers between devices: 132 us -> 0 us
  Pallas kernels: 0 us -> 115 us
  blocking collectives: 79.1 us -> 0 us
  waiting for transfers between devices: 54.4 us -> 0 us
  matrix products: 37.1 us -> 0 us
  local copies, waits for them, and re-layouts: 31.6 us -> 8.34 us
  between operations: 15.4 us -> 0.75 us
    scatter-add x1 -> x0, other arithmetic: 233 us -> none  [prepare_tables(): table_near = jnp.zeros((9 * atom_count * proj_count * cell_count,), jnp.f...]
    ppermute x44 -> x0, starting transfers between devices: 132 us -> none  [the longest x22 103 us: with_halo(): lax.ppermute(tail, axis, [(i, (i + 1) % count) for i in range(ends)])]
    pallas_call x0 -> x3, Pallas kernels: none -> 115 us  [the longest x1 49.9 us: per_device_whole(): pl.pallas_call(functools.partial(project_kernel, (dom_x, dom_y, bands, fl...]
    psum x2 -> x0, blocking collectives: 79.1 us -> none  [the longest x1 40.8 us: per_device(): lax.psum(lax.dynamic_update_slice(empty_square, over_cols, (0, band_start...]
    ppermute x44 -> x0, waiting for transfers between devices: 42.7 us -> none  [the longest x22 36.9 us: with_halo(): lax.ppermute(head, axis, [((i + 1) % count, i) for i in range(ends)])]
    dot_general x10 -> x0, matrix products: 36.9 us -> none  [the longest x3 19.1 us: apply_hamiltonian(): jnp.einsum('ijanc,ijanb->bc', table_near, near_coefs, precision=highest)]
    all_gather x1 -> x0, waiting for transfers between devices: 11.6 us -> none  [per_device(): whole_block = lax.all_gather(filt_flat, 'band', axis=0, tiled=True)]
    reshape x13 -> x1, local copies, waits for them, and re-layouts: 9.95 us -> 0.1 us  [per_device_whole(): coups = smalls[:, :atom_count * proj_count].reshape(atoms, proj_count, 1)]
  transfers between devices with their start and end apart: 45 -> 0, of which waited for: 11 -> 0; matrix products, arithmetic and copies ran while one was open for 7% -> 0% of each run, Pallas kernels for 0% -> 0%
where the time goes in v1:
time: 125 us
  Pallas kernels  115 us (92%)
  local copies, waits for them, and re-layouts  8.34 us (7%)
    pallas_call x1, Pallas kernels, per_device_whole(): pl.pallas_call(functools.partial(project_kernel, (dom_x, dom_y, bands, fl...  49.9 us
    pallas_call x1, Pallas kernels, per_device_whole(): pl.pallas_call(functools.partial(gather_kernel, (dom_x, dom_y)), out_shap...  41.1 us
    pallas_call x1, Pallas kernels, per_device_whole(): pl.pallas_call(functools.partial(compute_kernel, (count, atom_count, proj...  23.9 us
    unnamed x18, local copies, waits for them, and re-layouts  6.14 us

profile of v1, /device:TPU:0, one launch (start us, length us, event | category | flops | bytes accessed | tf_op | source)
XLA Modules:
  0.0 125.1 jit_solution(14671528644508781269)
XLA Ops:
  0.6 0.0 copy-start.6
  0.6 0.0 copy-start.5
  0.7 0.8 reshape_squeeze.7
  1.4 0.0 copy-done.6
  1.4 0.0 copy-start.4
  1.5 0.1 pad.11.clone
  1.5 0.1 select_maximum_fusion
  1.6 0.0 copy-done.5
  1.6 0.1 fusion.7
  1.7 0.5 copy-done.4
  2.2 0.7 maximum_maximum_fusion.pack_ref
  2.8 41.1 %shard_map.94 = (f32[4,8,4,8,128]{4,3,2,1,0:T(8,128)}, f32[4,8,4,8,128]{4,3,2,1,0:T(8,128)}, f32[16,16,512]{2,1,0:T(8,128)}) custom-call(f32[16,8,8,128]{3,2,1,0:T(8,128)} %orb_ref.1, f32[8,8,128]{2,1,0:T(8,128)} %pot_ref.1, f32[16,512]{1,0:T(8,128)} %maximum_maximum_fusion.pack_ref), custom_call_target="tpu_custom_call" | custom-call | tf_op jit(solution)/shard_map/pallas_call | solution.py:617
  43.9 1.0 slice.25
  44.9 0.1 fusion.1
  45.0 0.1 stack_reshape.9
  45.1 0.0 copy-start.3
  45.1 0.1 fusion.4
  45.2 0.1 add_select_fusion
  45.3 0.1 stack_reshape.11
  45.4 0.1 stack_reshape.10
  45.5 0.1 reshape.126.coup_ref
  45.6 0.4 copy-done.3
  46.0 0.0 copy-start
  46.0 1.0 copy-done
  47.0 0.0 copy-start.1
  47.0 1.0 copy-done.1
  48.0 0.0 copy-start.2
  48.0 1.0 copy-done.2
  49.1 23.9 %shard_map.95 = (f32[32,32,128]{2,1,0:T(8,128)S(1)}, f32[32,32,128]{2,1,0:T(8,128)S(1)}) custom-call(s32[3,32]{1,0:T(4,128)S(1)} %pad_add_fusion.home_ref, f32[32,32,128]{2,1,0:T(8,128)S(1)} %bitcast.28, f32[32,32,128]{2,1,0:T(8,128)S(1)} %bitcast.29, f32[16,16,512]{2,1,0:T(8,128)S(1)} %copy-done, f32[32,4,1]{2,1,0:T(4,128)S(1)} %reshape.126.coup_ref, ...), custom_call_target="tpu_custom_call" | custom-call | tf_op jit(solution)/shard_map/pallas_call | solution.py:647
  73.0 49.9 %shard_map.96 = (f32[16,2,4,8,128]{4,3,2,1,0:T(8,128)S(1)}, f32[16,2,4,8,128]{4,3,2,1,0:T(8,128)S(1)}, f32[32,32]{1,0:T(8,128)S(1)}) custom-call(f32[4,2,4,4,8,128]{5,4,3,2,1,0:T(8,128)S(1)} %bitcast.24, f32[4,2,4,4,8,128]{5,4,3,2,1,0:T(8,128)S(1)} %bitcast.25), custom_call_target="tpu_custom_call" | custom-call | tf_op jit(solution)/shard_map/pallas_call | solution.py:667
  122.9 0.8 copy.18
  123.7 0.8 copy.19
  124.5 0.6 copy.20
  (9 shorter events, 0.0 us)
Async XLA Ops:
  0.6 0.8 copy-start.6
  0.6 1.0 copy-start.5
  1.4 0.7 copy-start.4
  45.1 0.8 copy-start.3
  46.0 1.0 copy-start
  47.0 1.0 copy-start.1
  48.0 1.0 copy-start.2

commit v2 on v1

--- a/solution.py
+++ b/solution.py
@@ -199,11 +199,15 @@
 scale = -0.5 / spacing**2
 
 
-def gather_kernel(dims, orb_ref, pot_ref, pack_ref, orb_out, pot_out, pack_out, local_sem, send_sem, recv_sem):
-    dom_x, dom_y = dims
+def gather_kernel(
+    dims, orb_ref, pot_ref, pack_ref, orb_out, pot_out, pack_out, local_sem, send_sem, recv_sem, *stage_sems
+):
+    dom_x, dom_y, bands = dims
     count = dom_x * dom_y
-    my_x, my_y = lax.axis_index("gx"), lax.axis_index("gy")
+    my_x, my_y, my_band = lax.axis_index("gx"), lax.axis_index("gy"), lax.axis_index("band")
     me = my_x * dom_y + my_y
+    half = pot_ref.shape[0] // bands
+    mine = pl.ds(my_band * half, half)
 
     barrier = pltpu.get_barrier_semaphore()
 
@@ -214,61 +218,136 @@
         )
         return carry
 
-    def parts(peer, source_x, source_y):
-        source = source_x * dom_y + source_y
-        target = {"gx": peer // dom_y, "gy": lax.rem(peer, dom_y)}
-        pairs = (
-            (pack_ref, pack_out.at[source]),
-            (pot_ref, pot_out.at[source_x, :, source_y]),
-            (orb_ref.at[peer], orb_out.at[source_x, :, source_y]),
-        )
+    lax.fori_loop(1, count, greet, 0)
+    for step in range(1, bands):
+        pl.semaphore_signal(
+            barrier, inc=1, device_id={"band": lax.rem(my_band + step, bands)}, device_id_type=MESH
+        )
+
+    def orb_copy(peer, source):
+        return pltpu.make_async_remote_copy(
+            src_ref=orb_ref.at[peer],
+            dst_ref=orb_out.at[source // dom_y, :, lax.rem(source, dom_y)],
+            send_sem=send_sem.at[peer],
+            recv_sem=recv_sem.at[source],
+            device_id={"gx": peer // dom_y, "gy": lax.rem(peer, dom_y)},
+            device_id_type=MESH,
+        )
+
+    def stage_copies(stage, axis, peer, source):
+        if stage == 0:
+            pairs = (
+                (pack_ref.at[my_band], pack_out.at[my_x * dom_y + source, my_band]),
+                (pot_ref.at[mine], pot_out.at[my_x, mine, source]),
+            )
+        elif stage == 1:
+            block = pack_out.at[pl.ds(source * dom_y, dom_y), my_band]
+            strip = pot_out.at[source, mine]
+            pairs = ((block, block), (strip, strip))
+        else:
+            block = pack_out.at[:, source]
+            strip = pot_out.at[:, pl.ds(source * half, half)]
+            pairs = ((block, block), (strip, strip))
         return [
             pltpu.make_async_remote_copy(
                 src_ref=src,
                 dst_ref=dst,
-                send_sem=send_sem.at[kind, peer],
-                recv_sem=recv_sem.at[kind, source],
-                device_id=target,
+                send_sem=stage_sems[2 * stage].at[kind, peer],
+                recv_sem=stage_sems[2 * stage + 1].at[kind, source],
+                device_id={axis: peer},
                 device_id_type=MESH,
             )
             for kind, (src, dst) in enumerate(pairs)
         ]
 
-    lax.fori_loop(1, count, greet, 0)
+    def start_stage(stage, axis, place, size):
+        for step in range(1, size):
+            for copy in stage_copies(stage, axis, lax.rem(place + step, size), place):
+                copy.start()
+
+    def end_stage(stage, axis, place, size):
+        for step in range(1, size):
+            peer = lax.rem(place + step, size)
+            for copy in stage_copies(stage, axis, peer, place):
+                copy.wait_send()
+            for copy in stage_copies(stage, axis, peer, peer):
+                copy.wait_recv()
+
     own = [
-        pltpu.make_async_copy(pack_ref, pack_out.at[me], local_sem.at[0]),
-        pltpu.make_async_copy(pot_ref, pot_out.at[my_x, :, my_y], local_sem.at[1]),
+        pltpu.make_async_copy(pack_ref.at[my_band], pack_out.at[me, my_band], local_sem.at[0]),
+        pltpu.make_async_copy(pot_ref.at[mine], pot_out.at[my_x, mine, my_y], local_sem.at[1]),
         pltpu.make_async_copy(orb_ref.at[me], orb_out.at[my_x, :, my_y], local_sem.at[2]),
     ]
     for copy in own:
         copy.start()
-    pl.semaphore_wait(barrier, count - 1)
+    pl.semaphore_wait(barrier, count - 1 + bands - 1)
 
     def send(step, carry):
-        for copy in parts(lax.rem(me + step, count), my_x, my_y):
-            copy.start()
+        orb_copy(lax.rem(me + step, count), me).start()
         return carry
 
     def finish(step, carry):
         peer = lax.rem(me + step, count)
-        for copy in parts(peer, my_x, my_y):
-            copy.wait_send()
-        for copy in parts(peer, peer // dom_y, lax.rem(peer, dom_y)):
-            copy.wait_recv()
+        orb_copy(peer, me).wait_send()
+        orb_copy(peer, peer).wait_recv()
         return carry
 
-    lax.fori_loop(1, count, send, 0)
+    early = count // 4
+    start_stage(0, "gy", my_y, dom_y)
+    lax.fori_loop(1, early, send, 0)
+    end_stage(0, "gy", my_y, dom_y)
+    own[0].wait()
+    own[1].wait()
+    start_stage(1, "gx", my_x, dom_x)
+    lax.fori_loop(early, count, send, 0)
+    end_stage(1, "gx", my_x, dom_x)
+    start_stage(2, "band", my_band, bands)
+    end_stage(2, "band", my_band, bands)
     lax.fori_loop(1, count, finish, 0)
-    for copy in own:
-        copy.wait()
+    own[2].wait()
 
 
 def compute_kernel(
-    dims, home_ref, orb_ref, pot_ref, pack_ref, coup_ref, along_ref, filt_out, image_out, table, field, out, sums, coefs
+    dims,
+    orb_any,
+    pot_any,
+    pack_any,
+    along_ref,
+    filt_any,
+    image_any,
+    table,
+    field,
+    out,
+    sums,
+    coefs,
+    orb_ref,
+    pot_ref,
+    pack_ref,
+    small,
+    copy_sem,
 ):
-    count, atom_count, proj_count = dims
+    count, atom_count, proj_count, dom_y, size_x, size_y = dims
     nx, ny, nz = orb_ref.shape
-    points = pack_ref.shape[2]
+    points = pack_ref.shape[3]
+    fetch_pack = pltpu.make_async_copy(pack_any, pack_ref, copy_sem.at[0])
+    fetch_small = pltpu.make_async_copy(pack_any.at[:, :, proj_count + 1, pl.ds(0, 128)], small, copy_sem.at[1])
+    fetch_pack.start()
+    fetch_small.start()
+    field[...] = jnp.zeros_like(field)
+    inside_field = field.at[pl.ds(reach, nx), pl.ds(pad_y, ny), :]
+    fetch_field = pltpu.make_async_copy(orb_any, inside_field, copy_sem.at[2])
+    fetch_pot = pltpu.make_async_copy(pot_any, pot_ref, copy_sem.at[3])
+    fetch_orb = pltpu.make_async_copy(orb_any, orb_ref, copy_sem.at[4])
+    fetch_field.start()
+    fetch_pot.start()
+    fetch_orb.start()
+
+    def home_of(dom, atom):
+        cell = small[dom, atom, proj_count].astype(jnp.int32)
+        home_x = dom // dom_y * size_x + cell // (size_y * nz)
+        home_y = lax.rem(dom, dom_y) * size_y + lax.rem(cell // nz, size_y) + pad_y - reach
+        return home_x, home_y, lax.rem(cell, nz)
+
     rows = box * box_y
     wide = 16
     lane = lax.broadcasted_iota(jnp.int32, (rows, nz), 1)
@@ -277,12 +356,12 @@
 
     def build(dom, carry):
         for atom in range(atom_count):
-            cell = pack_ref[dom, 8 + atom : 9 + atom, :].astype(jnp.int32)
+            cell = pack_ref[dom, atom, proj_count : proj_count + 1, :].astype(jnp.int32)
             hot_xy = jnp.where(row_xy == lax.shift_right_arithmetic(cell, 4), 1.0, 0.0).astype(jnp.bfloat16)
             hot_z = row_z == (cell & 15)
             values = jnp.concatenate(
                 [
-                    jnp.where(hot_z, pack_ref[dom, proj_count * atom + n : proj_count * atom + n + 1, :], 0.0)
+                    jnp.where(hot_z, pack_ref[dom, atom, n : n + 1, :], 0.0)
                     for n in range(proj_count)
                 ],
                 axis=0,
@@ -293,22 +372,25 @@
             boxes = lax.dot_general(hot_xy, both, (((1,), (1,)), ((), ())), preferred_element_type=jnp.float32)
             boxes = boxes + pltpu.roll(boxes, proj_count * wide, 1)
             at = dom * atom_count + atom
-            low_z = home_ref[2, at] - reach
+            low_z = home_of(dom, atom)[2] - reach
             for n in range(proj_count):
                 kept = jnp.where((lane >= n * wide) & (lane < (n + 1) * wide), boxes, 0.0)
                 moved = pltpu.roll(kept, lax.rem(low_z - n * wide + 2 * nz, nz), 1)
                 table[at, n] = moved.reshape(box, box_y, nz)
         return carry
 
-    field[...] = jnp.zeros_like(field)
     out[...] = jnp.zeros_like(out)
     inner = pl.ds(pad_y, ny)
-    field[reach : reach + nx, pad_y : pad_y + ny, :] = orb_ref[...]
+    fetch_pack.wait()
+    fetch_small.wait()
     lax.fori_loop(0, count, build, 0)
+    fetch_field.wait()
+    fetch_pot.wait()
+    fetch_orb.wait()
 
     def hamiltonian():
         def project(at, carry):
-            x0, y0 = home_ref[0, at], home_ref[1, at]
+            x0, y0, _ = home_of(at // atom_count, lax.rem(at, atom_count))
             totals = [jnp.zeros((box_y, nz), jnp.float32) for _ in range(proj_count)]
             for dx in range(box):
                 part = field[x0 + dx, pl.ds(y0, box_y), :]
@@ -319,7 +401,7 @@
             return carry
 
         lax.fori_loop(0, count * atom_count, project, 0)
-        scaled = jnp.sum(sums[...], axis=2, keepdims=True) * coup_ref[...]
+        scaled = jnp.sum(sums[...], axis=2, keepdims=True)
         coefs[...] = jnp.broadcast_to(scaled, coefs.shape)
 
         chunk = 8
@@ -347,8 +429,13 @@
         lax.fori_loop(0, nx, stencil_row, 0)
 
         def spread(at, carry):
-            x0, y0 = home_ref[0, at], home_ref[1, at]
-            weights = [jnp.broadcast_to(coefs[at, n : n + 1, :], (box_y, nz)) for n in range(proj_count)]
+            x0, y0, _ = home_of(at // atom_count, lax.rem(at, atom_count))
+            weights = [
+                jnp.broadcast_to(
+                    coefs[at, n : n + 1, :] * small[at // atom_count, lax.rem(at, atom_count), n], (box_y, nz)
+                )
+                for n in range(proj_count)
+            ]
             for dx in range(box):
                 added = out[x0 + dx, pl.ds(y0, box_y), :]
                 for n in range(proj_count):
@@ -374,12 +461,17 @@
         at = row + reach
         value = (out[at, inner, :] - middle * field[at, inner, :]) * (2.0 / half_width) - orb_ref[row]
         field[at, inner, :] = value
-        filt_out[row] = value
+        orb_ref[row] = value
         return carry
 
     lax.fori_loop(0, nx, filter_row, 0)
+    store_filt = pltpu.make_async_copy(orb_ref, filt_any, copy_sem.at[5])
+    store_filt.start()
     hamiltonian()
-    image_out[...] = out[reach : reach + nx, pad_y : pad_y + ny, :]
+    store_image = pltpu.make_async_copy(out.at[pl.ds(reach, nx), pl.ds(pad_y, ny), :], image_any, copy_sem.at[6])
+    store_image.start()
+    store_filt.wait()
+    store_image.wait()
 
 
 def project_kernel(
@@ -448,86 +540,84 @@
         copy.start()
     pl.semaphore_wait(barrier, orbs - 1)
 
-    def send(step, carry):
-        for copy in parts(lax.rem(me + step, orbs), me):
-            copy.start()
-        return carry
-
-    def finish(step, carry):
-        peer = lax.rem(me + step, orbs)
-        for copy in parts(peer, me):
-            copy.wait_send()
-        for copy in parts(peer, peer):
-            copy.wait_recv()
-        return carry
-
-    lax.fori_loop(1, orbs, send, 0)
-    lax.fori_loop(1, orbs, finish, 0)
-    for copy in own:
-        copy.wait()
+    for kind in range(2):
+
+        def send(step, carry, kind=kind):
+            parts(lax.rem(me + step, orbs), me)[kind].start()
+            return carry
+
+        lax.fori_loop(1, orbs, send, 0)
+
+    def finish(kind):
+        def one(step, carry):
+            peer = lax.rem(me + step, orbs)
+            parts(peer, me)[kind].wait_send()
+            parts(peer, peer)[kind].wait_recv()
+            return carry
+
+        lax.fori_loop(1, orbs, one, 0)
+        own[kind].wait()
 
     flat = cells.reshape(2 * orbs * rows, cells.shape[3])
-    gram = jnp.zeros((orbs, 2 * orbs), jnp.float32)
-    for row in range(rows):
-        both = flat[pl.ds(row, 2 * orbs, stride=rows), :]
-        gram = gram + lax.dot_general(
-            both[:orbs],
-            both,
-            (((1,), (1,)), ((), ())),
-            precision=highest,
-            preferred_element_type=jnp.float32,
-        )
+    flat_result = result.reshape(2 * orbs * rows, cells.shape[3])
+
+    def product(left, right, dims_in):
+        return lax.dot_general(left, right, (dims_in, ((), ())), precision=highest, preferred_element_type=jnp.float32)
+
+    def load(ref, kind, row):
+        return ref[pl.ds(kind * orbs * rows + row, orbs, stride=rows), :]
 
     in_plane = dom_x * bands
     my_plane = my_x * bands + my_band
-    plane[my_plane] = gram
-
-    def plane_copy(peer, slot):
+
+    def plane_copy(kind, peer, slot):
         return pltpu.make_async_remote_copy(
-            src_ref=plane.at[my_plane],
-            dst_ref=plane.at[slot],
-            send_sem=plane_send.at[peer],
-            recv_sem=plane_recv.at[slot],
+            src_ref=plane.at[kind, my_plane],
+            dst_ref=plane.at[kind, slot],
+            send_sem=plane_send.at[kind, peer],
+            recv_sem=plane_recv.at[kind, slot],
             device_id={"gx": peer // bands, "gy": my_y, "band": lax.rem(peer, bands)},
             device_id_type=MESH,
         )
 
-    for step in range(1, in_plane):
-        plane_copy(lax.rem(my_plane + step, in_plane), my_plane).start()
-    for step in range(1, in_plane):
-        peer = lax.rem(my_plane + step, in_plane)
-        plane_copy(peer, my_plane).wait_send()
-        plane_copy(peer, peer).wait_recv()
-    total = plane[0]
-    for slot in range(1, in_plane):
-        total = total + plane[slot]
-    column[my_y] = total
-
-    def column_copy(peer, slot):
+    def column_copy(kind, peer, slot):
         return pltpu.make_async_remote_copy(
-            src_ref=column.at[my_y],
-            dst_ref=column.at[slot],
-            send_sem=column_send.at[peer],
-            recv_sem=column_recv.at[slot],
+            src_ref=column.at[kind, my_y],
+            dst_ref=column.at[kind, slot],
+            send_sem=column_send.at[kind, peer],
+            recv_sem=column_recv.at[kind, slot],
             device_id={"gx": my_x, "gy": peer, "band": my_band},
             device_id_type=MESH,
         )
 
-    for step in range(1, dom_y):
-        column_copy(lax.rem(my_y + step, dom_y), my_y).start()
-    for step in range(1, dom_y):
-        peer = lax.rem(my_y + step, dom_y)
-        column_copy(peer, my_y).wait_send()
-        column_copy(peer, peer).wait_recv()
-    total = column[0]
-    for slot in range(1, dom_y):
-        total = total + column[slot]
-    total = total * (1.0 / total_cells)
+    def summed(kind, share, box_ref, copy_of, place_at, size):
+        box_ref[kind, place_at] = share
+        for step in range(1, size):
+            copy_of(kind, lax.rem(place_at + step, size), place_at).start()
+        for step in range(1, size):
+            peer = lax.rem(place_at + step, size)
+            copy_of(kind, peer, place_at).wait_send()
+            copy_of(kind, peer, peer).wait_recv()
+        total = box_ref[kind, 0]
+        for slot in range(1, size):
+            total = total + box_ref[kind, slot]
+        return total
+
+    def all_sum(kind, share):
+        share = summed(kind, share, plane, plane_copy, my_plane, in_plane)
+        return summed(kind, share, column, column_copy, my_y, dom_y) * (1.0 / total_cells)
+
+    finish(0)
+    gram = jnp.zeros((orbs, orbs), jnp.float32)
+    for row in range(rows):
+        part = load(flat, 0, row)
+        gram = gram + product(part, part, ((1,), (1,)))
+    total = all_sum(0, gram)
 
     row_at = lax.broadcasted_iota(jnp.int32, (orbs, orbs), 0)
     col_at = lax.broadcasted_iota(jnp.int32, (orbs, orbs), 1)
     eye = jnp.where(row_at == col_at, 1.0, 0.0)
-    work = jnp.concatenate([total[:, :orbs], eye], axis=1)
+    work = jnp.concatenate([total, eye], axis=1)
     row_wide = lax.broadcasted_iota(jnp.int32, (orbs, 2 * orbs), 0)
     for k in range(orbs):
         pivot_row = work[k : k + 1, :]
@@ -537,31 +627,7 @@
     diagonal = jnp.sum(work[:, :orbs] * eye, axis=1, keepdims=True)
     inverse = work[:, orbs:] / jnp.sqrt(diagonal)
 
-    def product(left, right, dims_in):
-        return lax.dot_general(left, right, (dims_in, ((), ())), precision=highest, preferred_element_type=jnp.float32)
-
-    projected = product(inverse, total[:, orbs:], ((1,), (0,)))
-    subspace = product(projected, inverse, ((1,), (1,)))
-    sub_out[...] = subspace
-    half_width = 0.5 * (top_edge - low_edge)
-    mixed = product(subspace, inverse, ((0,), (0,))) * (-1.0 / half_width)
-    top = jnp.concatenate([inverse, jnp.zeros_like(inverse)], axis=1)
-    bottom = jnp.concatenate([mixed, inverse * (1.0 / half_width)], axis=1)
-    rotation = jnp.concatenate([top, bottom], axis=0)
-    flat_result = result.reshape(2 * orbs * rows, cells.shape[3])
-    for row in range(rows):
-        both = flat[pl.ds(row, 2 * orbs, stride=rows), :]
-        flat_result[pl.ds(row, 2 * orbs, stride=rows), :] = product(rotation, both, ((1,), (0,)))
-
     outs = (new_out, res_out)
-    keep = [
-        pltpu.make_async_copy(
-            result.at[pl.ds(kind * orbs + my_band * per_band, per_band)], out.at[:, my_band], out_sem.at[kind]
-        )
-        for kind, out in enumerate(outs)
-    ]
-    for copy in keep:
-        copy.start()
 
     def pair_copy(kind, other, half):
         return pltpu.make_async_remote_copy(
@@ -573,17 +639,41 @@
             device_id_type=MESH,
         )
 
-    for step in range(1, bands):
-        other = lax.rem(my_band + step, bands)
-        for kind in range(2):
-            pair_copy(kind, other, my_band).start()
-    for step in range(1, bands):
-        other = lax.rem(my_band + step, bands)
-        for kind in range(2):
+    def keep(kind):
+        source = result.at[pl.ds(kind * orbs + my_band * per_band, per_band)]
+        return pltpu.make_async_copy(source, outs[kind].at[:, my_band], out_sem.at[kind])
+
+    def give(kind):
+        for step in range(1, bands):
+            pair_copy(kind, lax.rem(my_band + step, bands), my_band).start()
+        keep(kind).start()
+
+    for row in range(rows):
+        flat_result[pl.ds(row, orbs, stride=rows), :] = product(inverse, load(flat, 0, row), ((1,), (0,)))
+    give(0)
+
+    finish(1)
+    gram = jnp.zeros((orbs, orbs), jnp.float32)
+    for row in range(rows):
+        gram = gram + product(load(flat, 0, row), load(flat, 1, row), ((1,), (1,)))
+    total = all_sum(1, gram)
+    projected = product(inverse, total, ((1,), (0,)))
+    subspace = product(projected, inverse, ((1,), (1,)))
+    sub_out[...] = subspace
+    half_width = 0.5 * (top_edge - low_edge)
+    mixed = product(subspace, inverse, ((0,), (0,))) * (-1.0 / half_width)
+    rotation = jnp.concatenate([mixed, inverse * (1.0 / half_width)], axis=1)
+    for row in range(rows):
+        both = jnp.concatenate([load(flat, 0, row), load(flat, 1, row)], axis=0)
+        flat_result[pl.ds(orbs * rows + row, orbs, stride=rows), :] = product(rotation, both, ((1,), (0,)))
+    give(1)
+
+    for kind in range(2):
+        for step in range(1, bands):
+            other = lax.rem(my_band + step, bands)
             pair_copy(kind, other, my_band).wait_send()
             pair_copy(kind, other, other).wait_recv()
-    for copy in keep:
-        copy.wait()
+        keep(kind).wait()
 
 
 def per_device_whole(orbitals, local_potential, atom_cell, support_offset, projector, coupling):
@@ -595,7 +685,6 @@
     atoms = count * atom_count
     any_spec = pl.BlockSpec(memory_space=pl.ANY)
     vmem = pl.BlockSpec(memory_space=pltpu.VMEM)
-    smem = pl.BlockSpec(memory_space=pltpu.SMEM)
 
     cell = atom_cell[0, 0]
     offset = support_offset[:, 0, 0]
@@ -603,41 +692,35 @@
     point_z = home_z[:, None] + offset[2]
     box_cell = ((offset[0] + reach) * box_y + offset[1] + reach) * 16 + offset[2] + reach
     box_cell = jnp.where((point_z >= 0) & (point_z < nz), box_cell, -1).astype(jnp.float32)
-    small = jnp.concatenate([coupling[0, 0].reshape(-1), cell.astype(jnp.float32)])
+    small = jnp.concatenate([coupling[0, 0], cell[:, None].astype(jnp.float32)], axis=1)
     pack = jnp.concatenate(
         [
-            projector[0, 0].reshape(atom_count * proj_count, points),
-            box_cell,
-            jnp.pad(small, (0, points - small.shape[0]))[None],
-            jnp.zeros((16 - atom_count * proj_count - atom_count - 1, points), jnp.float32),
+            projector[0, 0],
+            box_cell[:, None],
+            jnp.pad(small, ((0, 0), (0, points - small.shape[1])))[:, None],
+            jnp.zeros((atom_count, 8 - proj_count - 2, points), jnp.float32),
         ],
-        axis=0,
+        axis=1,
     )
     f32 = jnp.float32
     whole_orb, whole_pot, packs = pl.pallas_call(
-        functools.partial(gather_kernel, (dom_x, dom_y)),
+        functools.partial(gather_kernel, (dom_x, dom_y, bands)),
         out_shape=(
             jax.ShapeDtypeStruct((dom_x, size_x, dom_y, size_y, nz), f32),
             jax.ShapeDtypeStruct((dom_x, size_x, dom_y, size_y, nz), f32),
-            jax.ShapeDtypeStruct((count, 16, points), f32),
+            jax.ShapeDtypeStruct((count, atom_count, 8, points), f32),
         ),
         in_specs=[any_spec] * 3,
         out_specs=(any_spec,) * 3,
         scratch_shapes=[
             pltpu.SemaphoreType.DMA((3,)),
-            pltpu.SemaphoreType.DMA((3, count)),
-            pltpu.SemaphoreType.DMA((3, count)),
-        ],
+            pltpu.SemaphoreType.DMA((count,)),
+            pltpu.SemaphoreType.DMA((count,)),
+        ]
+        + [pltpu.SemaphoreType.DMA((2, size)) for size in (dom_y, dom_x, bands) for _ in range(2)],
         compiler_params=pltpu.CompilerParams(collective_id=0, has_side_effects=True),
     )(orbitals, local_potential, pack)
 
-    smalls = packs[:, atom_count * proj_count + atom_count, :]
-    coups = smalls[:, : atom_count * proj_count].reshape(atoms, proj_count, 1)
-    homes = smalls[:, atom_count * proj_count : atom_count * proj_count + atom_count].astype(jnp.int32)
-    dom = jnp.arange(count, dtype=jnp.int32)[:, None]
-    home_x = dom // dom_y * size_x + homes // (size_y * nz)
-    home_y = dom % dom_y * size_y + homes // nz % size_y + pad_y - reach
-    home = jnp.stack([home_x.reshape(-1), home_y.reshape(-1), (homes % nz).reshape(-1)])
     along = np.zeros((nz, nz), np.float32)
     for i in range(nz):
         for j in range(max(0, i - reach), min(nz, i + reach + 1)):
@@ -645,19 +728,24 @@
 
     field_shape = (nx + 2 * reach, ny + 2 * pad_y + 8, nz)
     filt, image = pl.pallas_call(
-        functools.partial(compute_kernel, (count, atom_count, proj_count)),
+        functools.partial(compute_kernel, (count, atom_count, proj_count, dom_y, size_x, size_y)),
         out_shape=(jax.ShapeDtypeStruct((nx, ny, nz), f32),) * 2,
-        in_specs=[smem] + [vmem] * 5,
-        out_specs=(vmem, vmem),
+        in_specs=[any_spec] * 3 + [vmem],
+        out_specs=(any_spec, any_spec),
         scratch_shapes=[
             pltpu.VMEM((atoms, proj_count, box, box_y, nz), f32),
             pltpu.VMEM(field_shape, f32),
             pltpu.VMEM(field_shape, f32),
             pltpu.VMEM((atoms, proj_count, nz), f32),
             pltpu.VMEM((atoms, proj_count, nz), f32),
+            pltpu.VMEM((nx, ny, nz), f32),
+            pltpu.VMEM((nx, ny, nz), f32),
+            pltpu.VMEM(packs.shape, f32),
+            pltpu.SMEM((count, atom_count, 128), f32),
+            pltpu.SemaphoreType.DMA((7,)),
         ],
         compiler_params=pltpu.CompilerParams(vmem_limit_bytes=48 << 20),
-    )(home, whole_orb.reshape(nx, ny, nz), whole_pot.reshape(nx, ny, nz), packs, coups, jnp.asarray(along))
+    )(whole_orb.reshape(nx, ny, nz), whole_pot.reshape(nx, ny, nz), packs, jnp.asarray(along))
 
     orbs = orb_count * bands
     half = size_x // bands
@@ -676,15 +764,15 @@
         scratch_shapes=[
             pltpu.VMEM((2 * orbs, half, size_y, nz), f32),
             pltpu.VMEM((2 * orbs, half, size_y, nz), f32),
-            pltpu.VMEM((dom_x * bands, orbs, 2 * orbs), f32),
-            pltpu.VMEM((dom_y, orbs, 2 * orbs), f32),
+            pltpu.VMEM((2, dom_x * bands, orbs, orbs), f32),
+            pltpu.VMEM((2, dom_y, orbs, orbs), f32),
             sem((2,)),
             sem((2, orbs)),
             sem((2, orbs)),
-            sem((dom_x * bands,)),
-            sem((dom_x * bands,)),
-            sem((dom_y,)),
-            sem((dom_y,)),
+            sem((2, dom_x * bands)),
+            sem((2, dom_x * bands)),
+            sem((2, dom_y)),
+            sem((2, dom_y)),
             sem((2,)),
             sem((2, bands)),
             sem((2, bands)),
@@ -698,7 +786,8 @@
 
 def per_device(orbitals, local_potential, atom_cell, support_offset, projector, coupling):
     domains = lax.axis_size("gx") * lax.axis_size("gy")
-    if orbitals.shape[0] == domains and orbitals.shape[1] % lax.axis_size("band") == 0:
+    bands = lax.axis_size("band")
+    if orbitals.shape[0] == domains and orbitals.shape[1] % bands == 0 and atom_cell.shape[2] == bands:
         plan = per_device_whole
     else:
         plan = per_device_halo

time: 125 us -> 112 us (0.90)
  Pallas kernels: 115 us -> 102 us
    pallas_call x1, Pallas kernels: 41.1 us -> 23.5 us  [per_device_whole(): pl.pallas_call(functools.partial(gather_kernel, (dom_x, dom_y, bands)), o...]
    pallas_call x1, Pallas kernels: 23.9 us -> 26.7 us  [per_device_whole(): pl.pallas_call(functools.partial(compute_kernel, (count, atom_count, proj...]
    pallas_call x1, Pallas kernels: 49.9 us -> 52.2 us  [per_device_whole(): pl.pallas_call(functools.partial(project_kernel, (dom_x, dom_y, bands, fl...]
    unnamed x18 -> x19, local copies, waits for them, and re-layouts: 6.14 us -> 7.03 us
where the time goes in v2:
time: 112 us; the launch traced here: 111 us
  Pallas kernels  102 us (91%)
  local copies, waits for them, and re-layouts  7.21 us (6%)
    pallas_call x1, Pallas kernels, per_device_whole(): pl.pallas_call(functools.partial(project_kernel, (dom_x, dom_y, bands, fl...  52.2 us
    pallas_call x1, Pallas kernels, per_device_whole(): pl.pallas_call(functools.partial(compute_kernel, (count, atom_count, proj...  26.7 us
    pallas_call x1, Pallas kernels, per_device_whole(): pl.pallas_call(functools.partial(gather_kernel, (dom_x, dom_y, bands)), o...  23.5 us
    unnamed x19, local copies, waits for them, and re-layouts  7.03 us

profile of v2, /device:TPU:0, one launch (start us, length us, event | category | flops | bytes accessed | tf_op | source)
XLA Modules:
  0.0 111.2 jit_solution(12219792861790342248)
XLA Ops:
  0.6 0.0 copy-start.7
  0.6 0.0 copy-start.6
  0.7 0.6 copy-done.7
  1.3 0.0 copy-start.5
  1.3 0.1 copy.13
  1.4 0.1 pad.8.clone
  1.5 0.0 copy-done.6
  1.5 0.1 select_maximum_fusion
  1.6 0.4 copy-done.5
  2.0 0.0 copy-start.4
  2.0 0.1 fusion.3
  2.1 0.6 copy-done.4
  2.7 0.7 maximum_maximum_fusion.pack_ref
  3.4 0.0 copy-start.3
  3.4 23.5 %shard_map.94 = (f32[4,8,4,8,128]{4,3,2,1,0:T(8,128)}, f32[4,8,4,8,128]{4,3,2,1,0:T(8,128)}, f32[16,2,8,512]{3,2,1,0:T(8,128)}) custom-call(f32[16,8,8,128]{3,2,1,0:T(8,128)} %orb_ref.1, f32[8,8,128]{2,1,0:T(8,128)} %pot_ref.1, f32[2,8,512]{2,1,0:T(8,128)} %maximum_maximum_fusion.pack_ref), custom_call_target="tpu_custom_call" | custom-call | tf_op jit(solution)/shard_map/pallas_call | solution.py:706
  26.9 0.0 copy-done.3
  26.9 0.0 copy-start
  26.9 1.0 copy-done
  27.9 0.0 copy-start.1
  27.9 1.0 copy-done.1
  29.0 0.0 copy-start.2
  29.0 1.0 copy-done.2
  30.0 26.7 %shard_map.95 = (f32[32,32,128]{2,1,0:T(8,128)S(1)}, f32[32,32,128]{2,1,0:T(8,128)S(1)}) custom-call(f32[32,32,128]{2,1,0:T(8,128)S(1)} %bitcast.26, f32[32,32,128]{2,1,0:T(8,128)S(1)} %bitcast.27, f32[16,2,8,512]{3,2,1,0:T(8,128)S(1)} %copy-done.2, f32[128,128]{1,0:T(8,128)S(1)} %copy-done.3), custom_call_target="tpu_custom_call" | custom-call | tf_op jit(solution)/shard_map/pallas_call | solution.py:730
  56.7 52.2 %shard_map.96 = (f32[16,2,4,8,128]{4,3,2,1,0:T(8,128)S(1)}, f32[16,2,4,8,128]{4,3,2,1,0:T(8,128)S(1)}, f32[32,32]{1,0:T(8,128)S(1)}) custom-call(f32[4,2,4,4,8,128]{5,4,3,2,1,0:T(8,128)S(1)} %bitcast.28, f32[4,2,4,4,8,128]{5,4,3,2,1,0:T(8,128)S(1)} %bitcast.29), custom_call_target="tpu_custom_call" | custom-call | tf_op jit(solution)/shard_map/pallas_call | solution.py:755
  109.0 0.8 copy.41
  109.8 0.8 copy.42
  110.6 0.6 copy.43
  (5 shorter events, 0.0 us)
Async XLA Ops:
  0.6 0.7 copy-start.7
  0.6 0.8 copy-start.6
  1.3 0.7 copy-start.5
  2.0 0.7 copy-start.4
  3.4 23.5 %copy-start.3 = (f32[128,128]{1,0:T(8,128)S(1)}, f32[128,128]{1,0:T(8,128)}, u32[]{:S(2)}) copy-start(f32[128,128]{1,0:T(8,128)} %constant.29.clone.along_ref) | copy-start | bytes 196612
  26.9 1.0 copy-start
  27.9 1.0 copy-start.1
  29.0 1.0 copy-start.2

commit v3 on v2

--- a/solution.py
+++ b/solution.py
@@ -383,7 +383,7 @@
     inner = pl.ds(pad_y, ny)
     fetch_pack.wait()
     fetch_small.wait()
-    lax.fori_loop(0, count, build, 0)
+    lax.fori_loop(0, count, build, 0, unroll=2)
     fetch_field.wait()
     fetch_pot.wait()
     fetch_orb.wait()
@@ -400,7 +400,7 @@
             sums[at] = jnp.concatenate(stacked, axis=0)
             return carry
 
-        lax.fori_loop(0, count * atom_count, project, 0)
+        lax.fori_loop(0, count * atom_count, project, 0, unroll=2)
         scaled = jnp.sum(sums[...], axis=2, keepdims=True)
         coefs[...] = jnp.broadcast_to(scaled, coefs.shape)
 
@@ -426,7 +426,7 @@
             out[at, inner, :] = summed
             return carry
 
-        lax.fori_loop(0, nx, stencil_row, 0)
+        lax.fori_loop(0, nx, stencil_row, 0, unroll=2)
 
         def spread(at, carry):
             x0, y0, _ = home_of(at // atom_count, lax.rem(at, atom_count))
@@ -570,49 +570,64 @@
     in_plane = dom_x * bands
     my_plane = my_x * bands + my_band
 
-    def plane_copy(kind, peer, slot):
+    def plane_copy(peer, slot):
         return pltpu.make_async_remote_copy(
-            src_ref=plane.at[kind, my_plane],
-            dst_ref=plane.at[kind, slot],
-            send_sem=plane_send.at[kind, peer],
-            recv_sem=plane_recv.at[kind, slot],
+            src_ref=plane.at[my_plane],
+            dst_ref=plane.at[slot],
+            send_sem=plane_send.at[peer],
+            recv_sem=plane_recv.at[slot],
             device_id={"gx": peer // bands, "gy": my_y, "band": lax.rem(peer, bands)},
             device_id_type=MESH,
         )
 
-    def column_copy(kind, peer, slot):
+    def column_copy(peer, slot):
         return pltpu.make_async_remote_copy(
-            src_ref=column.at[kind, my_y],
-            dst_ref=column.at[kind, slot],
-            send_sem=column_send.at[kind, peer],
-            recv_sem=column_recv.at[kind, slot],
+            src_ref=column.at[my_y],
+            dst_ref=column.at[slot],
+            send_sem=column_send.at[peer],
+            recv_sem=column_recv.at[slot],
             device_id={"gx": my_x, "gy": peer, "band": my_band},
             device_id_type=MESH,
         )
 
-    def summed(kind, share, box_ref, copy_of, place_at, size):
-        box_ref[kind, place_at] = share
+    def summed(share, box_ref, copy_of, place_at, size):
+        box_ref[place_at] = share
         for step in range(1, size):
-            copy_of(kind, lax.rem(place_at + step, size), place_at).start()
+            copy_of(lax.rem(place_at + step, size), place_at).start()
         for step in range(1, size):
             peer = lax.rem(place_at + step, size)
-            copy_of(kind, peer, place_at).wait_send()
-            copy_of(kind, peer, peer).wait_recv()
-        total = box_ref[kind, 0]
+            copy_of(peer, place_at).wait_send()
+            copy_of(peer, peer).wait_recv()
+        total = box_ref[0]
         for slot in range(1, size):
-            total = total + box_ref[kind, slot]
+            total = total + box_ref[slot]
         return total
 
-    def all_sum(kind, share):
-        share = summed(kind, share, plane, plane_copy, my_plane, in_plane)
-        return summed(kind, share, column, column_copy, my_y, dom_y) * (1.0 / total_cells)
+    def all_sum(share):
+        share = summed(share, plane, plane_copy, my_plane, in_plane)
+        return summed(share, column, column_copy, my_y, dom_y) * (1.0 / total_cells)
+
+    sums_across = plane.shape[1] // 2
+    groups = orbs // sums_across
+
+    def dense(square):
+        return jnp.concatenate([square[g * sums_across : (g + 1) * sums_across] for g in range(groups)], axis=1)
+
+    def square_of(packed):
+        return jnp.concatenate([packed[:, g * orbs : (g + 1) * orbs] for g in range(groups)], axis=0)
 
     finish(0)
     gram = jnp.zeros((orbs, orbs), jnp.float32)
     for row in range(rows):
         part = load(flat, 0, row)
         gram = gram + product(part, part, ((1,), (1,)))
-    total = all_sum(0, gram)
+    finish(1)
+    mixed_gram = jnp.zeros((orbs, orbs), jnp.float32)
+    for row in range(rows):
+        mixed_gram = mixed_gram + product(load(flat, 0, row), load(flat, 1, row), ((1,), (1,)))
+    totals = all_sum(jnp.concatenate([dense(gram), dense(mixed_gram)], axis=0))
+    total = square_of(totals[:sums_across])
+    crossed = square_of(totals[sums_across:])
 
     row_at = lax.broadcasted_iota(jnp.int32, (orbs, orbs), 0)
     col_at = lax.broadcasted_iota(jnp.int32, (orbs, orbs), 1)
@@ -652,12 +667,7 @@
         flat_result[pl.ds(row, orbs, stride=rows), :] = product(inverse, load(flat, 0, row), ((1,), (0,)))
     give(0)
 
-    finish(1)
-    gram = jnp.zeros((orbs, orbs), jnp.float32)
-    for row in range(rows):
-        gram = gram + product(load(flat, 0, row), load(flat, 1, row), ((1,), (1,)))
-    total = all_sum(1, gram)
-    projected = product(inverse, total, ((1,), (0,)))
+    projected = product(inverse, crossed, ((1,), (0,)))
     subspace = product(projected, inverse, ((1,), (1,)))
     sub_out[...] = subspace
     half_width = 0.5 * (top_edge - low_edge)
@@ -748,6 +758,7 @@
     )(whole_orb.reshape(nx, ny, nz), whole_pot.reshape(nx, ny, nz), packs, jnp.asarray(along))
 
     orbs = orb_count * bands
+    sum_rows = orbs // max(1, nz // orbs)
     half = size_x // bands
     rows = half * size_y
     shape = (dom_x, bands, half, dom_y, size_y, nz)
@@ -764,15 +775,15 @@
         scratch_shapes=[
             pltpu.VMEM((2 * orbs, half, size_y, nz), f32),
             pltpu.VMEM((2 * orbs, half, size_y, nz), f32),
-            pltpu.VMEM((2, dom_x * bands, orbs, orbs), f32),
-            pltpu.VMEM((2, dom_y, orbs, orbs), f32),
+            pltpu.VMEM((dom_x * bands, 2 * sum_rows, orbs * orbs // sum_rows), f32),
+            pltpu.VMEM((dom_y, 2 * sum_rows, orbs * orbs // sum_rows), f32),
             sem((2,)),
             sem((2, orbs)),
             sem((2, orbs)),
-            sem((2, dom_x * bands)),
-            sem((2, dom_x * bands)),
-            sem((2, dom_y)),
-            sem((2, dom_y)),
+            sem((dom_x * bands,)),
+            sem((dom_x * bands,)),
+            sem((dom_y,)),
+            sem((dom_y,)),
             sem((2,)),
             sem((2, bands)),
             sem((2, bands)),

time: 112 us -> 103 us (0.920)
  Pallas kernels: 102 us -> 93.7 us
    pallas_call x1, Pallas kernels: 52.2 us -> 47.9 us  [per_device_whole(): pl.pallas_call(functools.partial(project_kernel, (dom_x, dom_y, bands, fl...]
    pallas_call x1, Pallas kernels: 26.7 us -> 22.4 us  [per_device_whole(): pl.pallas_call(functools.partial(compute_kernel, (count, atom_count, proj...]
where the time goes in v3:
time: 103 us; the launch traced here: 102 us
  Pallas kernels  93.7 us (91%)
  local copies, waits for them, and re-layouts  7.21 us (7%)
    pallas_call x1, Pallas kernels, per_device_whole(): pl.pallas_call(functools.partial(project_kernel, (dom_x, dom_y, bands, fl...  47.9 us
    pallas_call x1, Pallas kernels, per_device_whole(): pl.pallas_call(functools.partial(gather_kernel, (dom_x, dom_y, bands)), o...  23.5 us
    pallas_call x1, Pallas kernels, per_device_whole(): pl.pallas_call(functools.partial(compute_kernel, (count, atom_count, proj...  22.4 us
    unnamed x19, local copies, waits for them, and re-layouts  7.03 us

profile of v3, /device:TPU:0, one launch (start us, length us, event | category | flops | bytes accessed | tf_op | source)
XLA Modules:
  0.0 102.5 jit_solution(15603095899828726775)
XLA Ops:
  0.6 0.0 copy-start.7
  0.6 0.0 copy-start.6
  0.7 0.6 copy-done.7
  1.3 0.0 copy-start.5
  1.3 0.1 copy.13
  1.4 0.1 pad.8.clone
  1.5 0.0 copy-done.6
  1.5 0.1 select_maximum_fusion
  1.6 0.4 copy-done.5
  2.0 0.0 copy-start.4
  2.0 0.1 fusion.3
  2.1 0.6 copy-done.4
  2.7 0.7 maximum_maximum_fusion.pack_ref
  3.4 0.0 copy-start.3
  3.4 23.5 %shard_map.94 = (f32[4,8,4,8,128]{4,3,2,1,0:T(8,128)}, f32[4,8,4,8,128]{4,3,2,1,0:T(8,128)}, f32[16,2,8,512]{3,2,1,0:T(8,128)}) custom-call(f32[16,8,8,128]{3,2,1,0:T(8,128)} %orb_ref.1, f32[8,8,128]{2,1,0:T(8,128)} %pot_ref.1, f32[2,8,512]{2,1,0:T(8,128)} %maximum_maximum_fusion.pack_ref), custom_call_target="tpu_custom_call" | custom-call | tf_op jit(solution)/shard_map/pallas_call | solution.py:716
  26.9 0.0 copy-done.3
  26.9 0.0 copy-start
  26.9 1.0 %copy-done = f32[4,8,4,8,128]{4,3,2,1,0:T(8,128)S(1)} copy-done((f32[4,8,4,8,128]{4,3,2,1,0:T(8,128)S(1)}, f32[4,8,4,8,128]{4,3,2,1,0:T(8,128)}, u32[]{:S(2)}) %copy-start) | copy-done | bytes 524312
  27.9 0.0 copy-start.1
  27.9 1.0 %copy-done.1 = f32[4,8,4,8,128]{4,3,2,1,0:T(8,128)S(1)} copy-done((f32[4,8,4,8,128]{4,3,2,1,0:T(8,128)S(1)}, f32[4,8,4,8,128]{4,3,2,1,0:T(8,128)}, u32[]{:S(2)}) %copy-start.1) | copy-done | bytes 524312
  29.0 0.0 copy-start.2
  29.0 1.0 %copy-done.2 = f32[16,2,8,512]{3,2,1,0:T(8,128)S(1)} copy-done((f32[16,2,8,512]{3,2,1,0:T(8,128)S(1)}, f32[16,2,8,512]{3,2,1,0:T(8,128)}, u32[]{:S(2)}) %copy-start.2) | copy-done | bytes 524312
  30.0 22.4 %shard_map.95 = (f32[32,32,128]{2,1,0:T(8,128)S(1)}, f32[32,32,128]{2,1,0:T(8,128)S(1)}) custom-call(f32[32,32,128]{2,1,0:T(8,128)S(1)} %bitcast.26, f32[32,32,128]{2,1,0:T(8,128)S(1)} %bitcast.27, f32[16,2,8,512]{3,2,1,0:T(8,128)S(1)} %copy-done.2, f32[128,128]{1,0:T(8,128)S(1)} %copy-done.3), custom_call_target="tpu_custom_call" | custom-call | tf_op jit(solution)/shard_map/pallas_call | solution.py:740
  52.4 47.9 %shard_map.96 = (f32[16,2,4,8,128]{4,3,2,1,0:T(8,128)S(1)}, f32[16,2,4,8,128]{4,3,2,1,0:T(8,128)S(1)}, f32[32,32]{1,0:T(8,128)S(1)}) custom-call(f32[4,2,4,4,8,128]{5,4,3,2,1,0:T(8,128)S(1)} %bitcast.28, f32[4,2,4,4,8,128]{5,4,3,2,1,0:T(8,128)S(1)} %bitcast.29), custom_call_target="tpu_custom_call" | custom-call | tf_op jit(solution)/shard_map/pallas_call | solution.py:766
  100.3 0.8 copy.41
  101.1 0.8 copy.42
  101.9 0.6 copy.43
  (5 shorter events, 0.0 us)
Async XLA Ops:
  0.6 0.7 copy-start.7
  0.6 0.8 copy-start.6
  1.3 0.7 copy-start.5
  2.0 0.7 copy-start.4
  3.4 23.5 %copy-start.3 = (f32[128,128]{1,0:T(8,128)S(1)}, f32[128,128]{1,0:T(8,128)}, u32[]{:S(2)}) copy-start(f32[128,128]{1,0:T(8,128)} %constant.29.clone.along_ref) | copy-start | bytes 196612
  26.9 1.0 %copy-start = (f32[4,8,4,8,128]{4,3,2,1,0:T(8,128)S(1)}, f32[4,8,4,8,128]{4,3,2,1,0:T(8,128)}, u32[]{:S(2)}) copy-start(f32[4,8,4,8,128]{4,3,2,1,0:T(8,128)} %get-tuple-element.11) | copy-start | bytes 1572868
  27.9 1.0 %copy-start.1 = (f32[4,8,4,8,128]{4,3,2,1,0:T(8,128)S(1)}, f32[4,8,4,8,128]{4,3,2,1,0:T(8,128)}, u32[]{:S(2)}) copy-start(f32[4,8,4,8,128]{4,3,2,1,0:T(8,128)} %get-tuple-element.12) | copy-start | bytes 1572868
  29.0 1.0 %copy-start.2 = (f32[16,2,8,512]{3,2,1,0:T(8,128)S(1)}, f32[16,2,8,512]{3,2,1,0:T(8,128)}, u32[]{:S(2)}) copy-start(f32[16,2,8,512]{3,2,1,0:T(8,128)} %get-tuple-element.13.pack_any) | copy-start | bytes 1572868

commit v4 on v3

--- a/solution.py
+++ b/solution.py
@@ -383,7 +383,7 @@
     inner = pl.ds(pad_y, ny)
     fetch_pack.wait()
     fetch_small.wait()
-    lax.fori_loop(0, count, build, 0, unroll=2)
+    lax.fori_loop(0, count, build, 0, unroll=4)
     fetch_field.wait()
     fetch_pot.wait()
     fetch_orb.wait()
@@ -400,7 +400,7 @@
             sums[at] = jnp.concatenate(stacked, axis=0)
             return carry
 
-        lax.fori_loop(0, count * atom_count, project, 0, unroll=2)
+        lax.fori_loop(0, count * atom_count, project, 0, unroll=4)
         scaled = jnp.sum(sums[...], axis=2, keepdims=True)
         coefs[...] = jnp.broadcast_to(scaled, coefs.shape)
 
@@ -426,7 +426,7 @@
             out[at, inner, :] = summed
             return carry
 
-        lax.fori_loop(0, nx, stencil_row, 0, unroll=2)
+        lax.fori_loop(0, nx, stencil_row, 0, unroll=4)
 
         def spread(at, carry):
             x0, y0, _ = home_of(at // atom_count, lax.rem(at, atom_count))
@@ -443,7 +443,7 @@
                 out[x0 + dx, pl.ds(y0, box_y), :] = added
             return carry
 
-        lax.fori_loop(0, count * atom_count, spread, 0)
+        lax.fori_loop(0, count * atom_count, spread, 0, unroll=2)
 
     middle = 0.5 * (top_edge + low_edge)
     half_width = 0.5 * (top_edge - low_edge)
@@ -454,7 +454,7 @@
         field[at, inner, :] = (out[at, inner, :] - middle * field[at, inner, :]) * (1.0 / half_width)
         return carry
 
-    lax.fori_loop(0, nx, first_row, 0)
+    lax.fori_loop(0, nx, first_row, 0, unroll=4)
     hamiltonian()
 
     def filter_row(row, carry):
@@ -464,7 +464,7 @@
         orb_ref[row] = value
         return carry
 
-    lax.fori_loop(0, nx, filter_row, 0)
+    lax.fori_loop(0, nx, filter_row, 0, unroll=4)
     store_filt = pltpu.make_async_copy(orb_ref, filt_any, copy_sem.at[5])
     store_filt.start()
     hamiltonian()

time: 103 us -> 100 us (0.971)
  Pallas kernels: 93.7 us -> 91 us
    pallas_call x1, Pallas kernels: 22.4 us -> 19.6 us  [per_device_whole(): pl.pallas_call(functools.partial(compute_kernel, (count, atom_count, proj...]
where the time goes in v4:
time: 100 us; the launch traced here: 99.7 us
  Pallas kernels  91 us (91%)
  local copies, waits for them, and re-layouts  7.21 us (7%)
    pallas_call x1, Pallas kernels, per_device_whole(): pl.pallas_call(functools.partial(project_kernel, (dom_x, dom_y, bands, fl...  47.8 us
    pallas_call x1, Pallas kernels, per_device_whole(): pl.pallas_call(functools.partial(gather_kernel, (dom_x, dom_y, bands)), o...  23.5 us
    pallas_call x1, Pallas kernels, per_device_whole(): pl.pallas_call(functools.partial(compute_kernel, (count, atom_count, proj...  19.6 us
    unnamed x19, local copies, waits for them, and re-layouts  7.03 us

profile of v4, /device:TPU:0, one launch (start us, length us, event | category | flops | bytes accessed | tf_op | source)
XLA Modules:
  0.0 99.7 jit_solution(12276465556316359416)
XLA Ops:
  0.6 0.0 copy-start.7
  0.6 0.0 copy-start.6
  0.7 0.6 copy-done.7
  1.3 0.0 copy-start.5
  1.3 0.1 copy.13
  1.4 0.1 pad.8.clone
  1.5 0.0 copy-done.6
  1.5 0.1 select_maximum_fusion
  1.6 0.4 copy-done.5
  2.0 0.0 copy-start.4
  2.0 0.1 fusion.3
  2.1 0.6 copy-done.4
  2.7 0.7 maximum_maximum_fusion.pack_ref
  3.4 0.0 copy-start.3
  3.4 23.5 %shard_map.94 = (f32[4,8,4,8,128]{4,3,2,1,0:T(8,128)}, f32[4,8,4,8,128]{4,3,2,1,0:T(8,128)}, f32[16,2,8,512]{3,2,1,0:T(8,128)}) custom-call(f32[16,8,8,128]{3,2,1,0:T(8,128)} %orb_ref.1, f32[8,8,128]{2,1,0:T(8,128)} %pot_ref.1, f32[2,8,512]{2,1,0:T(8,128)} %maximum_maximum_fusion.pack_ref), custom_call_target="tpu_custom_call" | custom-call | tf_op jit(solution)/shard_map/pallas_call | solution.py:716
  26.9 0.0 copy-done.3
  26.9 0.0 copy-start
  26.9 1.0 %copy-done = f32[4,8,4,8,128]{4,3,2,1,0:T(8,128)S(1)} copy-done((f32[4,8,4,8,128]{4,3,2,1,0:T(8,128)S(1)}, f32[4,8,4,8,128]{4,3,2,1,0:T(8,128)}, u32[]{:S(2)}) %copy-start) | copy-done | bytes 524312
  27.9 0.0 copy-start.1
  27.9 1.0 %copy-done.1 = f32[4,8,4,8,128]{4,3,2,1,0:T(8,128)S(1)} copy-done((f32[4,8,4,8,128]{4,3,2,1,0:T(8,128)S(1)}, f32[4,8,4,8,128]{4,3,2,1,0:T(8,128)}, u32[]{:S(2)}) %copy-start.1) | copy-done | bytes 524312
  29.0 0.0 copy-start.2
  29.0 1.0 %copy-done.2 = f32[16,2,8,512]{3,2,1,0:T(8,128)S(1)} copy-done((f32[16,2,8,512]{3,2,1,0:T(8,128)S(1)}, f32[16,2,8,512]{3,2,1,0:T(8,128)}, u32[]{:S(2)}) %copy-start.2) | copy-done | bytes 524312
  30.0 19.6 %shard_map.95 = (f32[32,32,128]{2,1,0:T(8,128)S(1)}, f32[32,32,128]{2,1,0:T(8,128)S(1)}) custom-call(f32[32,32,128]{2,1,0:T(8,128)S(1)} %bitcast.26, f32[32,32,128]{2,1,0:T(8,128)S(1)} %bitcast.27, f32[16,2,8,512]{3,2,1,0:T(8,128)S(1)} %copy-done.2, f32[128,128]{1,0:T(8,128)S(1)} %copy-done.3), custom_call_target="tpu_custom_call" | custom-call | tf_op jit(solution)/shard_map/pallas_call | solution.py:740
  49.7 47.8 %shard_map.96 = (f32[16,2,4,8,128]{4,3,2,1,0:T(8,128)S(1)}, f32[16,2,4,8,128]{4,3,2,1,0:T(8,128)S(1)}, f32[32,32]{1,0:T(8,128)S(1)}) custom-call(f32[4,2,4,4,8,128]{5,4,3,2,1,0:T(8,128)S(1)} %bitcast.28, f32[4,2,4,4,8,128]{5,4,3,2,1,0:T(8,128)S(1)} %bitcast.29), custom_call_target="tpu_custom_call" | custom-call | tf_op jit(solution)/shard_map/pallas_call | solution.py:766
  97.5 0.8 copy.41
  98.3 0.8 copy.42
  99.1 0.6 copy.43
  (5 shorter events, 0.0 us)
Async XLA Ops:
  0.6 0.7 copy-start.7
  0.6 0.8 copy-start.6
  1.3 0.7 copy-start.5
  2.0 0.7 copy-start.4
  3.4 23.5 %copy-start.3 = (f32[128,128]{1,0:T(8,128)S(1)}, f32[128,128]{1,0:T(8,128)}, u32[]{:S(2)}) copy-start(f32[128,128]{1,0:T(8,128)} %constant.29.clone.along_ref) | copy-start | bytes 196612
  26.9 1.0 %copy-start = (f32[4,8,4,8,128]{4,3,2,1,0:T(8,128)S(1)}, f32[4,8,4,8,128]{4,3,2,1,0:T(8,128)}, u32[]{:S(2)}) copy-start(f32[4,8,4,8,128]{4,3,2,1,0:T(8,128)} %get-tuple-element.11) | copy-start | bytes 1572868
  27.9 1.0 %copy-start.1 = (f32[4,8,4,8,128]{4,3,2,1,0:T(8,128)S(1)}, f32[4,8,4,8,128]{4,3,2,1,0:T(8,128)}, u32[]{:S(2)}) copy-start(f32[4,8,4,8,128]{4,3,2,1,0:T(8,128)} %get-tuple-element.12) | copy-start | bytes 1572868
  29.0 1.0 %copy-start.2 = (f32[16,2,8,512]{3,2,1,0:T(8,128)S(1)}, f32[16,2,8,512]{3,2,1,0:T(8,128)}, u32[]{:S(2)}) copy-start(f32[16,2,8,512]{3,2,1,0:T(8,128)} %get-tuple-element.13.pack_any) | copy-start | bytes 1572868
